TPU v7x, 256 devices: a whole 4x4x8 slice. The times are simulated.
256 devices in a mesh: section: 8 (over z), tile: 32 (over y, x, core).
Axes of the slice: x: 4, y: 4, z: 8, core: 2. Of those that a mesh axis runs over, the one named last changes fastest.
Arguments:
- frames_in: bfloat16 [8, 2, 32, 8, 60, 384], P('section', None, 'tile'), may hold values from -22 to 22
- cache: bfloat16 [8, 2, 32, 8, 60, 384], P('section', None, 'tile'), may hold values from -6 to 6
- kernel: bfloat16 [8, 3, 3, 3, 384, 384], P('section'), may hold values from -0.25 to 0.25
- gain: float32 [8, 384], P('section'), may hold values from 0.1 to 1.9
- conv_bias: float32 [8, 384], P('section'), may hold values from -3 to 3
Outputs:
- handed: bfloat16 [8, 2, 32, 8, 60, 384], P('section', None, 'tile')
- new_cache: bfloat16 [8, 2, 32, 8, 60, 384], P('section', None, 'tile')
All inputs are finite; a program needn't handle non-finite values.
Results may differ from a plain program's by a relative error of at most 0.0031.
Values may be sent and summed in bfloat16 or wider, within the bound.
No kernel may reach another device: no remote copies, remote signals or barrier semaphores. Data moves between devices by JAX's collectives and lax.ppermute only.
A program may use at most 128 MiB of HBM per device.

v0:
```python
import jax
import jax.numpy as jnp
from jax import lax
from jax.sharding import PartitionSpec as P

GROUPS = 32
TCOL = 4


EPS = 1e-06


def shifted(value, axis, steps):
    count = lax.axis_size(axis)
    first, last = (max(0, -steps), min(count, count - steps))
    return lax.ppermute(value, axis, [(source, source + steps) for source in range(first, last)])


def passed_along(x, axis, by):
    size = lax.axis_size(axis)
    return lax.ppermute(x, axis, [(i, (i + by) % size) for i in range(size)])


def activate(values, mean, var, scale_gain):
    frames, rows, width, chans = values.shape
    grouped = values.reshape(frames, rows, width, GROUPS, chans // GROUPS)
    scaled = (grouped - mean[:, None, None, :, None]) * lax.rsqrt(var[:, None, None, :, None] + EPS)
    return jax.nn.silu(scaled.reshape(frames, rows, width, chans) * scale_gain).astype(jnp.bfloat16)


def convolve(padded, weights, frames, rows, width):
    chans = padded.shape[-1]
    total = jnp.zeros((frames * rows * width, weights.shape[-1]), jnp.float32)
    for step_t in range(3):
        for step_h in range(3):
            block = padded[step_t : step_t + frames, step_h : step_h + rows]
            taps = jnp.concatenate(
                [block[:, :, step_w : step_w + width] for step_w in range(3)], axis=-1
            )
            taps = taps.reshape(-1, 3 * chans)
            matrix = weights[step_t, step_h].reshape(3 * chans, -1)
            total = total + jnp.dot(taps, matrix, preferred_element_type=jnp.float32)
    return total


def column_piece(piece, offset):
    return shifted(piece, "tile", offset)


def row_piece(piece, offset):
    return shifted(piece, "tile", offset)


def border(field):
    col_block = lax.axis_index("tile") % TCOL
    left = column_piece(field[:, :, -1:], 1)
    right = column_piece(field[:, :, :1], -1)
    left = jnp.where(col_block > 0, left, jnp.zeros_like(left))
    right = jnp.where(col_block < TCOL - 1, right, jnp.zeros_like(right))
    wide = jnp.concatenate([left, field, right], axis=2)
    above = row_piece(wide[:, -1:], TCOL)
    below = row_piece(wide[:, :1], -TCOL)
    return jnp.concatenate([above, wide, below], axis=1)


def on_device(frames_in, cache, kernel, gain, conv_bias):
    local_in = frames_in[0][:, 0]
    local_cache = cache[0][:, 0]
    values = local_in.astype(jnp.float32)
    frames, rows, width, chans = values.shape
    tiles = lax.axis_size("tile")
    count = rows * tiles * width * (chans // GROUPS)
    grouped = values.reshape(frames, rows, width, GROUPS, chans // GROUPS)
    mean = lax.psum(jnp.sum(grouped, axis=(1, 2, 4)), "tile") / count
    deviation = grouped - mean[:, None, None, :, None]
    var = lax.psum(jnp.sum(deviation * deviation, axis=(1, 2, 4)), "tile") / count
    scale_gain = gain[0]
    act = activate(values, mean, var, scale_gain)
    ext = jnp.concatenate([local_cache, act], axis=0)
    padded = border(ext)
    total = convolve(padded, kernel[0], frames, rows, width)
    result = (values + conv_bias[0] + total.reshape(frames, rows, width, chans)).astype(
        jnp.bfloat16
    )
    handed = passed_along(result[None, :, None], "section", 1)
    return (handed, ext[-2:][None, :, None])


def solution(mesh):
    in_specs = (
        P("section", None, "tile", None, None, None),
        P("section", None, "tile", None, None, None),
        P("section", None, None, None, None, None),
        P("section", None),
        P("section", None),
    )
    out_specs = (
        P("section", None, "tile", None, None, None),
        P("section", None, "tile", None, None, None),
    )
    return jax.shard_map(
        on_device, mesh=mesh, in_specs=in_specs, out_specs=out_specs, check_vma=False
    )
```

profile of v0, /device:TPU:1, one launch (start us, length us, event | category | flops | bytes accessed | tf_op | source)
XLA Modules:
  0.0 253.2 jit_solution(14721988853139436416)
XLA Ops:
  0.7 1.3 convert_reduce_fusion
  2.2 65.3 %psum.14 = f32[2,32]{1,0:T(2,128)S(1)} all-reduce(f32[2,32]{1,0:T(2,128)S(1)} %reduce_sum.25), channel_id=1, replica_groups=mesh['section'=8,'tile'=32] {'tile'}, use_global_device_ids=true, to_apply=%region_2.0 | all-reduce | flops 64 | bytes 512 | tf_op jit(solution)/shard_map/psum | solution.py:74
  67.7 1.3 fusion.10
  69.2 65.6 %psum.15 = f32[2,32]{1,0:T(2,128)S(1)} all-reduce(f32[2,32]{1,0:T(2,128)S(1)} %reduce_sum.37), channel_id=1, replica_groups=mesh['section'=8,'tile'=32] {'tile'}, use_global_device_ids=true, to_apply=%region_5.6 | all-reduce | flops 64 | bytes 512 | tf_op jit(solution)/shard_map/psum | solution.py:76
  135.2 0.5 fusion.28
  135.8 2.6 %collective-permute-start.1 = (bf16[4,8,1,384]{3,2,1,0:T(2,128)(2,1)S(1)}, bf16[4,8,1,384]{3,2,1,0:T(2,128)(2,1)S(1)}, u32[]{:S(2)}, u32[]{:S(2)}) collective-permute-start(bf16[4,8,1,384]{3,2,1,0:T(2,128)(2,1)S(1)} %get-tuple-element.46), channel_id=1, source_target_pairs={{1,0},{2,1},{3,2},{4,3},{5,4},{6,5},{7,6},{8,7},{9,8},{10,9},{11,1... | collective-permute-start | bytes 73736 | tf_op jit(solution)/shard_map/ppermute | solution.py:16
  138.3 3.0 %collective-permute-start = (bf16[4,8,1,384]{3,2,1,0:T(2,128)(2,1)S(1)}, bf16[4,8,1,384]{3,2,1,0:T(2,128)(2,1)S(1)}, u32[]{:S(2)}, u32[]{:S(2)}) collective-permute-start(bf16[4,8,1,384]{3,2,1,0:T(2,128)(2,1)S(1)} %get-tuple-element.45), channel_id=1, source_target_pairs={{0,1},{1,2},{2,3},{3,4},{4,5},{5,6},{6,7},{7,8},{8,9},{9,10},{10,1... | collective-permute-start | bytes 73736 | tf_op jit(solution)/shard_map/ppermute | solution.py:16
  141.4 5.7 %fusion.30 = (bf16[1,1,3,384,384]{4,3,2,1,0:T(8,128)(2,1)}, bf16[1,1,3,384,384]{4,3,2,1,0:T(8,128)(2,1)}, bf16[1,1,3,384,384]{4,3,2,1,0:T(8,128)(2,1)}, bf16[1,1...) fusion(bf16[3,3,3,384,384]{4,3,2,1,0:T(8,128)(2,1)} %bitcast.58), kind=kLoop, calls=%fused_computation.58 | loop fusion | bytes 15925248 | tf_op jit(solution)/shard_map/slice | solution.py:41
  147.1 1.0 concatenate.67
  148.2 0.9 pad_maximum_fusion.10
  149.1 1.1 maximum_maximum_fusion.1
  150.2 1.3 collective-permute-start.2
  151.5 1.5 collective-permute-start.3
  153.0 2.2 fusion.33
  155.3 2.0 concatenate.66
  157.3 2.0 concatenate.69
  159.3 3.7 %fusion.1 = (bf16[2,8,60,1152]{3,2,1,0:T(8,128)(2,1)}, bf16[2,8,60,1152]{3,2,1,0:T(8,128)(2,1)}) fusion(bf16[2,8,60,384]{3,2,1,0:T(8,128)(2,1)S(1)} %fusion.28, bf16[2,8,60,384]{3,2,1,0:T(8,128)(2,1)S(1)} %bitcast.56, bf16[2,8,60,384]{3,2,1,0:T(8,128)(2,1)} %get-tuple-element.53, bf16[2,8,60,384]{3,2,1,0:T(8,128)(2,1)} %get-tuple-element.39, ...), kind=kLoop, calls=%fused_computation.6 | loop fusion | flops 15482880 | bytes 8847360 | tf_op jit(solution)/shard_map/concatenate | solution.py:37
  163.0 4.0 %reshape.58 = bf16[960,1152]{1,0:T(8,128)(2,1)} reshape(bf16[2,8,60,1152]{3,2,1,0:T(8,128)(2,1)} %get-tuple-element.47) | data formatting | bytes 4423680 | tf_op jit(solution)/shard_map/reshape | solution.py:40
  167.0 4.1 %reshape.61 = bf16[960,1152]{1,0:T(8,128)(2,1)} reshape(bf16[2,8,60,1152]{3,2,1,0:T(8,128)(2,1)} %get-tuple-element.48) | data formatting | bytes 4423680 | tf_op jit(solution)/shard_map/reshape | solution.py:40
  171.2 4.3 %fusion.39 = f32[960,384]{1,0:T(8,128)} fusion(bf16[960,1152]{1,0:T(8,128)(2,1)} %reshape.58, bf16[1152,384]{1,0:T(8,128)(2,1)S(1)} %bitcast.67), kind=kOutput, calls=%fused_computation.67 | convolution fusion | flops 849346560 | bytes 4571136 | tf_op jit(solution)/shard_map/dot_general | solution.py:42
  175.5 2.5 fusion.2
  178.0 2.5 %fusion.42 = f32[960,384]{1,0:T(8,128)} fusion(bf16[960,1152]{1,0:T(8,128)(2,1)S(1)} %copy-done.7, bf16[1152,384]{1,0:T(8,128)(2,1)S(1)} %bitcast.65), kind=kOutput, calls=%fused_computation.70 | convolution fusion | flops 849346560 | bytes 4571136 | tf_op jit(solution)/shard_map/dot_general | solution.py:42
  180.5 4.9 %pad_maximum_fusion.8 = (bf16[4,9,62,384]{3,2,1,0:T(8,128)(2,1)S(1)}, bf16[4,9,62,384]{3,2,1,0:T(8,128)(2,1)S(1)}) fusion(bf16[4,1,62,384]{3,2,1,0:T(8,128)(2,1)} %collective-permute-done.3, bf16[4,8,1,384]{3,2,1,0:T(2,128)(2,1)S(1)} %broadcast_select_fusion, bf16[2,8,60,384]{3,2,1,0:T(8,128)(2,1)S(1)} %fusion.28, bf16[2,8,60,384]{3,2,1,0:T(8,128)(2,1)S(1)} %bitcast.57, ...), kind=kLoop, calls=%fused_computation.23 | loop fusion | flops 17141760 | bytes 5332992 | tf_op jit(solution)/shard_map/concatenate | solution.py:63
  185.4 5.5 %fusion.31 = (bf16[2,8,60,384]{3,2,1,0:T(8,128)(2,1)S(1)}, bf16[2,8,60,384]{3,2,1,0:T(8,128)(2,1)S(1)}, bf16[2,8,60,384]{3,2,1,0:T(8,128)(2,1)S(1)}, bf16[2,8,60...) fusion(bf16[4,9,62,384]{3,2,1,0:T(8,128)(2,1)S(1)} %get-tuple-e, ...), kind=kLoop, calls=%fused_computation.59 | loop fusion | bytes 26542080 | tf_op jit(solution)/shard_map/slice | solution.py:38
  191.3 2.0 reshape.62
  193.3 1.9 pad_maximum_fusion.1
  195.2 2.1 reshape.55
  197.3 1.9 pad_maximum_fusion.2
  199.2 2.1 reshape.56
  201.3 1.9 pad_maximum_fusion.3
  203.3 2.1 reshape.57
  205.3 1.9 pad_maximum_fusion.4
  207.3 2.1 reshape.59
  209.3 1.9 pad_maximum_fusion.5
  211.3 2.1 reshape.60
  213.4 3.3 %fusion.36 = f32[960,384]{1,0:T(8,128)S(1)} fusion(bf16[960,1152]{1,0:T(8,128)(2,1)} %reshape.55, bf16[1152,384]{1,0:T(8,128)(2,1)} %bitcast.64), kind=kOutput, calls=%fused_computation.64 | convolution fusion | flops 849346560 | bytes 4571136 | tf_op jit(solution)/shard_map/dot_general | solution.py:42
  216.7 1.4 fusion.37
  218.6 1.4 fusion.38
  220.4 1.4 fusion.40
  222.2 1.4 fusion.41
  224.2 0.5 copy-done.8
  225.1 2.7 %add_add_fusion = f32[960,384]{1,0:T(8,128)} fusion(f32[960,384]{1,0:T(8,128)S(1)} %copy-done.10, f32[960,384]{1,0:T(8,128)S(1)} %fusion.41, f32[960,384]{1,0:T(8,128)S(1)} %fusion.40, f32[960,384]{1,0:T(8,128)S(1)} %copy-done.8, f32[960,384]{1,0:T(8,128)S(1)} %fusion.38, f32[960,384]{1,0:T(8,128)S(1)} %fusion.37, f32[960,384]{1,0:T(8,128)S(1)} %fusion.36, ...), kind=kOutput, calls=%fused_computation.45 | convolution fusion | flops 852295680 | bytes 16367616 | tf_op jit(solution)/shard_map/dot_general | solution.py:42
  227.8 1.4 reshape.63
  229.3 0.7 fusion.17
  230.4 1.7 collective-permute-start.4
  232.1 1.3 copy.17
  233.4 19.0 %collective-permute-done.4 = bf16[1,2,1,8,60,384]{5,3,4,2,1,0:T(8,128)(2,1)S(1)} collective-permute-done((bf16[1,2,1,8,60,384]{5,3,4,2,1,0:T(8,128)(2,1)S(1)}, bf16[1,2,1,8,60,384]{5,3,4,2,1,0:T(8,128)(2,1)S(1)}, u32[]{:S(2)}, u32[]{:S(2)}) %collective-permute-start.4) | collective-permute-done | bytes 737312 | tf_op jit(solution)/shard_map/ppermute | solution.py:21
  252.4 0.9 copy.27
  (69 shorter events, 4.4 us)
Async XLA Ops:
  0.6 134.5 %copy-start = (bf16[1,2,1,8,60,384]{5,3,4,2,1,0:T(8,128)(2,1)S(1)}, bf16[1,2,1,8,60,384]{5,3,4,2,1,0:T(8,128)(2,1)}, u32[]{:S(2)}) copy-start(bf16[1,2,1,8,60,384]{5,3,4,2,1,0:T(8,128)(2,1)} %param.5) | copy-start | bytes 2211844
  0.6 134.3 %copy-start.18 = (bf16[1,2,1,8,60,384]{5,3,4,2,1,0:T(8,128)(2,1)S(1)}, bf16[1,2,1,8,60,384]{5,3,4,2,1,0:T(8,128)(2,1)}, u32[]{:S(2)}) copy-start(bf16[1,2,1,8,60,384]{5,3,4,2,1,0:T(8,128)(2,1)} %param.6) | copy-start | bytes 2211844
  0.7 134.5 %copy-start.22 = (f32[1,384]{1,0:T(1,128)S(1)}, f32[1,384]{1,0:T(1,128)}, u32[]{:S(2)}) copy-start(f32[1,384]{1,0:T(1,128)} %param.8) | copy-start | bytes 4612
  135.8 12.3 %collective-permute-start.1 = (bf16[4,8,1,384]{3,2,1,0:T(2,128)(2,1)S(1)}, bf16[4,8,1,384]{3,2,1,0:T(2,128)(2,1)S(1)}, u32[]{:S(2)}, u32[]{:S(2)}) collective-permute-start(bf16[4,8,1,384]{3,2,1,0:T(2,128)(2,1)S(1)} %get-tuple-element.46), channel_id=1, source_target_pairs={{1,0},{2,1},{3,2},{4,3},{5,4},{6,5},{7,6},{8,7},{9,8},{10,9},{11,1... | collective-permute-start | bytes 73736 | tf_op jit(solution)/shard_map/ppermute | solution.py:16
  138.3 9.8 %collective-permute-start = (bf16[4,8,1,384]{3,2,1,0:T(2,128)(2,1)S(1)}, bf16[4,8,1,384]{3,2,1,0:T(2,128)(2,1)S(1)}, u32[]{:S(2)}, u32[]{:S(2)}) collective-permute-start(bf16[4,8,1,384]{3,2,1,0:T(2,128)(2,1)S(1)} %get-tuple-element.45), channel_id=1, source_target_pairs={{0,1},{1,2},{2,3},{3,4},{4,5},{5,6},{6,7},{7,8},{8,9},{9,10},{10,1... | collective-permute-start | bytes 73736 | tf_op jit(solution)/shard_map/ppermute | solution.py:16
  141.3 6.7 %copy-start.23 = (f32[1,384]{1,0:T(1,128)S(1)}, f32[1,384]{1,0:T(1,128)}, u32[]{:S(2)}) copy-start(f32[1,384]{1,0:T(1,128)} %param.9) | copy-start | bytes 4612
  150.2 30.3 %collective-permute-start.2 = (bf16[4,1,62,384]{3,2,1,0:T(8,128)(2,1)}, bf16[4,1,62,384]{3,2,1,0:T(8,128)(2,1)S(1)}, u32[]{:S(2)}, u32[]{:S(2)}) collective-permute-start(bf16[4,1,62,384]{3,2,1,0:T(8,128)(2,1)} %get-tuple-element.36), channel_id=1, source_target_pairs={{0,4},{1,5},{2,6},{3,7},{4,8},{5,9},{6,10},{7,11},{8,12},{9,13},{1... | collective-permute-start | bytes 571400 | tf_op jit(solution)/shard_map/ppermute | solution.py:16
  151.5 29.0 %collective-permute-start.3 = (bf16[4,1,62,384]{3,2,1,0:T(8,128)(2,1)}, bf16[4,1,62,384]{3,2,1,0:T(8,128)(2,1)}, u32[]{:S(2)}, u32[]{:S(2)}) collective-permute-start(bf16[4,1,62,384]{3,2,1,0:T(8,128)(2,1)} %get-tuple-element.35), channel_id=1, source_target_pairs={{4,0},{5,1},{6,2},{7,3},{8,4},{9,5},{10,6},{11,7},{12,8},{13,9},{1... | collective-permute-start | bytes 571400 | tf_op jit(solution)/shard_map/ppermute | solution.py:16
  167.0 4.1 %copy-start.17 = (bf16[1,1,3,384,384]{4,3,2,1,0:T(8,128)(2,1)S(1)}, bf16[1,1,3,384,384]{4,3,2,1,0:T(8,128)(2,1)}, u32[]{:S(2)}) copy-start(bf16[1,1,3,384,384]{4,3,2,1,0:T(8,128)(2,1)} %get-tuple-element.10) | copy-start | bytes 2654212
  171.1 4.3 %copy-start.16 = (bf16[1,1,3,384,384]{4,3,2,1,0:T(8,128)(2,1)S(1)}, bf16[1,1,3,384,384]{4,3,2,1,0:T(8,128)(2,1)}, u32[]{:S(2)}) copy-start(bf16[1,1,3,384,384]{4,3,2,1,0:T(8,128)(2,1)} %get-tuple-element.13) | copy-start | bytes 2654212
  171.1 4.3 %copy-start.19 = (bf16[960,384]{1,0:T(8,128)(2,1)S(1)}, bf16[960,384]{1,0:T(8,128)(2,1)}, u32[]{:S(2)}) copy-start(bf16[960,384]{1,0:T(8,128)(2,1)} %concatenate.67) | copy-start | bytes 2211844
  171.1 4.3 %copy-start.20 = (bf16[960,384]{1,0:T(8,128)(2,1)S(1)}, bf16[960,384]{1,0:T(8,128)(2,1)}, u32[]{:S(2)}) copy-start(bf16[960,384]{1,0:T(8,128)(2,1)} %concatenate.66) | copy-start | bytes 2211844
  171.2 4.3 %copy-start.21 = (bf16[960,384]{1,0:T(8,128)(2,1)S(1)}, bf16[960,384]{1,0:T(8,128)(2,1)}, u32[]{:S(2)}) copy-start(bf16[960,384]{1,0:T(8,128)(2,1)} %concatenate.69) | copy-start | bytes 2211844
  175.5 2.5 copy-start.7
  175.5 2.5 copy-start.15
  213.4 3.4 %copy-start.3 = (bf16[960,1152]{1,0:T(8,128)(2,1)S(1)}, bf16[960,1152]{1,0:T(8,128)(2,1)}, u32[]{:S(2)}) copy-start(bf16[960,1152]{1,0:T(8,128)(2,1)} %reshape.56) | copy-start | bytes 6635524
  213.4 3.4 %copy-start.14 = (bf16[1,1,3,384,384]{4,3,2,1,0:T(8,128)(2,1)S(1)}, bf16[1,1,3,384,384]{4,3,2,1,0:T(8,128)(2,1)}, u32[]{:S(2)}) copy-start(bf16[1,1,3,384,384]{4,3,2,1,0:T(8,128)(2,1)} %get-tuple-element.12) | copy-start | bytes 2654212
  216.7 1.6 copy-start.4
  216.7 1.8 copy-start.13
  218.6 1.6 copy-start.5
  218.6 1.8 copy-start.12
  220.4 1.6 copy-start.6
  220.4 1.8 copy-start.11
  220.4 3.2 %copy-start.10 = (f32[960,384]{1,0:T(8,128)S(1)}, f32[960,384]{1,0:T(8,128)}, u32[]{:S(2)}) copy-start(f32[960,384]{1,0:T(8,128)} %fusion.42) | copy-start | bytes 4423684
  222.2 1.7 copy-start.1
  222.2 1.9 copy-start.2
  222.2 2.4 copy-start.8
  222.2 2.8 %copy-start.9 = (f32[960,384]{1,0:T(8,128)S(1)}, f32[960,384]{1,0:T(8,128)}, u32[]{:S(2)}) copy-start(f32[960,384]{1,0:T(8,128)} %fusion.2) | copy-start | bytes 4423684
  230.4 22.0 %collective-permute-start.4 = (bf16[1,2,1,8,60,384]{5,3,4,2,1,0:T(8,128)(2,1)S(1)}, bf16[1,2,1,8,60,384]{5,3,4,2,1,0:T(8,128)(2,1)S(1)}, u32[]{:S(2)}, u32[]{:S(2)}) collective-permute-start(bf16[1,2,1,8,60,384]{5,3,4,2,1,0:T(8,128)(2,1)S(1)} %copy.16), channel_id=1, source_target_pairs={{0,32},{32,64},{64,96},{96,128},{128,160},{160,192},{192,224},{224... | collective-permute-start | bytes 2211848 | tf_op jit(solution)/shard_map/ppermute | solution.py:21
where the time goes:
time: 254 us; the launch traced here: 253 us
  blocking collectives  131 us (52%)
  local copies, waits for them, and re-layouts  46.7 us (18%)
  other arithmetic  24.7 us (10%)
  matrix products  20.8 us (8%)
  waiting for transfers between devices  19 us (7%)
  starting transfers between devices  10.1 us (4%)
    psum x1, blocking collectives, on_device(): lax.psum(jnp.sum(deviation * deviation, axis=(1, 2, 4)), 'tile') / count  65.6 us
    psum x1, blocking collectives, on_device(): mean = lax.psum(jnp.sum(grouped, axis=(1, 2, 4)), 'tile') / count  65.3 us
    dot_general x9, matrix products, convolve(): total = total + jnp.dot(taps, matrix, preferred_element_type=jnp.float32)  20.8 us
    reshape x8, local copies, waits for them, and re-layouts, convolve(): taps = taps.reshape(-1, 3 * chans)  20.6 us
    ppermute x1, waiting for transfers between devices, passed_along(): return lax.ppermute(x, axis, [(i, (i + by) % size) for i in range(size)])  19 us
    concatenate x7, other arithmetic, convolve(): jnp.concatenate([block[:, :, step_w:step_w + width] for step_w in range(3...  13.6 us
    ppermute x4, starting transfers between devices, shifted(): lax.ppermute(value, axis, [(source, source + steps) for source in range(f...  8.34 us
    slice x2, local copies, waits for them, and re-layouts, convolve(): block[:, :, step_w:step_w + width]  7.73 us
  transfers between devices with their start and end apart: 5, of which 1 were waited for; matrix products, arithmetic and copies ran while one was open for 14% of the time, Pallas kernels for 0%

commit v1 on v0

v1 whole, which is shorter than its diff:
```python
import functools

import jax
import jax.numpy as jnp
from jax import lax
from jax.experimental import pallas as pl
from jax.experimental.pallas import tpu as pltpu
from jax.sharding import PartitionSpec as P

GROUPS = 32
TCOL = 4
EPS = 1e-06
WP = 64
F32 = jnp.float32
BF16 = jnp.bfloat16
VMEM = pl.BlockSpec(memory_space=pltpu.VMEM)
ANY = pl.BlockSpec(memory_space=pl.ANY)
LIMIT = 20 * 1024 * 1024


def params():
    return pltpu.CompilerParams(vmem_limit_bytes=LIMIT)


def split3(x):
    high = x.astype(BF16)
    rest = x - high.astype(F32)
    mid = rest.astype(BF16)
    low = (rest - mid.astype(F32)).astype(BF16)
    return high, mid, low


def exact_dot(x, onehot):
    pad = jnp.zeros_like(x)
    parts = split3(x)
    lhs = jnp.concatenate([jnp.concatenate([p.astype(F32), pad], axis=0) for p in parts], axis=0)
    got = jnp.dot(lhs.astype(BF16), onehot, preferred_element_type=F32)
    return got[0:8] + got[16:24] + got[32:40]


def to_group(chans, block):
    size = chans // GROUPS
    chan = lax.broadcasted_iota(jnp.int32, (chans, 128), 0)
    lane = lax.broadcasted_iota(jnp.int32, (chans, 128), 1)
    first = (lane & (GROUPS - 1)) * size
    hit = (chan >= first) & (chan < first + size)
    if block is not None:
        hit = hit & ((lane >> 5) == block)
    return jnp.where(hit, 1.0, 0.0).astype(BF16)


def from_group(chans, block):
    size = chans // GROUPS
    lane = lax.broadcasted_iota(jnp.int32, (128, chans), 0)
    chan = lax.broadcasted_iota(jnp.int32, (128, chans), 1)
    first = (lane & (GROUPS - 1)) * size
    hit = (chan >= first) & (chan < first + size) & ((lane >> 5) == block)
    return jnp.where(hit, 1.0, 0.0).astype(BF16)


def first_kernel(x_ref, c_ref, stat_ref, send_a_ref, send_b_ref, left_scr, right_scr):
    frames, rows, width, chans = x_ref.shape
    size = chans // GROUPS
    count = rows * width
    odd = (lax.axis_index("tile") & 1) == 1
    for k in range(4):
        src = c_ref if k < 2 else x_ref
        for r in range(rows):
            left_scr[k * rows + r : k * rows + r + 1, :] = src[k % 2, r, 0:1, :].astype(F32)
            right_scr[k * rows + r : k * rows + r + 1, :] = src[k % 2, r, width - 1 : width, :].astype(F32)
    left, right = left_scr[...], right_scr[...]
    send_a_ref[...] = jnp.where(odd, left, right).astype(BF16)
    send_b_ref[...] = jnp.where(odd, right, left).astype(BF16)
    sums, squares = [], []
    for f in range(frames):
        x = x_ref[f].astype(F32)
        total = jnp.sum(jnp.sum(x, axis=0), axis=0, keepdims=True)
        dev = x - (total * (1.0 / count))[None]
        sums.append(total)
        squares.append(jnp.sum(jnp.sum(dev * dev, axis=0), axis=0, keepdims=True))
    zero = jnp.zeros((1, chans), F32)
    both = jnp.concatenate(sums + [zero] * 6, axis=0)
    grouped = exact_dot(both, to_group(chans, 0))
    spread = exact_dot(grouped, from_group(chans, 0))
    off = both * (1.0 / count) - spread * (1.0 / (count * size))
    square = jnp.concatenate(squares + [zero] * 6, axis=0) + count * off * off
    row = lax.broadcasted_iota(jnp.int32, (8, 128), 0)
    lane = lax.broadcasted_iota(jnp.int32, (8, 128), 1)
    every = to_group(chans, None)
    mix_sum = exact_dot(both, every)
    mix_square = exact_dot(square, every)
    kind = lane >> 5
    mixed = jnp.where((row == 0) & (kind == 0), mix_sum, 0.0)
    mixed = mixed + jnp.where((row == 1) & (kind == 2), mix_sum, 0.0)
    mixed = mixed + jnp.where((row == 0) & (kind == 1), mix_square, 0.0)
    mixed = mixed + jnp.where((row == 1) & (kind == 3), mix_square, 0.0)
    line = jnp.sum(mixed, axis=0, keepdims=True)
    stat_ref[...] = jnp.broadcast_to(line[None], stat_ref.shape)


def build_taps(frame, left, right, pad_ref, out_ref, rows):
    width, chans = frame.shape[1], frame.shape[2]
    pad_ref[:rows, 8 : 8 + width, :] = frame
    for r in range(rows):
        pad_ref[r, 7:8, :] = left[r : r + 1]
        pad_ref[r, 8 + width : 9 + width, :] = right[r : r + 1]
    for b in range(3):
        out_ref[:rows, :, b * chans : (b + 1) * chans] = pad_ref[:rows, 7 + b : 7 + b + WP, :].astype(BF16)


def cache_kernel(c_ref, x_ref, recv_a_ref, recv_b_ref, w_ref,
                 v_ref, x0_ref, x1_ref, acc0_ref, acc1_ref, top_ref, bottom_ref, left_ref, right_ref,
                 pad_ref, row_scr, sems):
    _, rows, width, chans = c_ref.shape
    copies = {}
    for a in range(3):
        for t in (0, 1):
            copies[t, a] = pltpu.make_async_copy(
                w_ref.at[t, a], v_ref.at[a, :, (2 - t) * chans : (3 - t) * chans], sems.at[t, a])
            copies[t, a].start()
    for a in range(3):
        copies[2, a] = pltpu.make_async_copy(w_ref.at[2, a], v_ref.at[a, :, 0:chans], sems.at[2, a])
        copies[2, a].start()
    odd = (lax.axis_index("tile") & 1) == 1
    got_a, got_b = recv_a_ref[...].astype(F32), recv_b_ref[...].astype(F32)
    left_ref[...] = jnp.where(odd, got_a, got_b)
    right_ref[...] = jnp.where(odd, got_b, got_a)
    pad_ref[...] = jnp.zeros_like(pad_ref)
    for k, out_ref in ((0, x0_ref), (1, x1_ref)):
        build_taps(c_ref[k].astype(F32), left_ref[k * rows : (k + 1) * rows], right_ref[k * rows : (k + 1) * rows],
                   pad_ref, out_ref, rows)
    for out_ref, r in ((top_ref, 0), (bottom_ref, rows - 1)):
        for k in range(4):
            src = c_ref if k < 2 else x_ref
            row_scr[...] = jnp.zeros_like(row_scr)
            row_scr[0:width, :] = src[k % 2, r].astype(F32)
            row_scr[width : width + 1, :] = left_ref[k * rows + r : k * rows + r + 1]
            row_scr[width + 1 : width + 2, :] = right_ref[k * rows + r : k * rows + r + 1]
            out_ref[k] = row_scr[...].astype(BF16)
    inner = rows - 2
    acc0 = jnp.zeros((inner * WP, chans), F32)
    acc1 = jnp.zeros((inner * WP, chans), F32)
    for a in range(3):
        copies[0, a].wait()
        copies[1, a].wait()
        lhs0 = x0_ref[a : a + inner].reshape(inner * WP, 3 * chans)
        lhs1 = x1_ref[a : a + inner].reshape(inner * WP, 3 * chans)
        acc0 = acc0 + jnp.dot(lhs0, v_ref[a, :, 2 * chans : 3 * chans], preferred_element_type=F32)
        part = jnp.dot(lhs1, v_ref[a, :, chans : 3 * chans], preferred_element_type=F32)
        acc0 = acc0 + part[:, :chans]
        acc1 = acc1 + part[:, chans:]
    acc0_ref[...] = acc0
    acc1_ref[...] = acc1
    for a in range(3):
        copies[2, a].wait()


def tile_place():
    tile = lax.axis_index("tile")
    return lax.div(tile, TCOL), lax.rem(tile, TCOL)


def silu(v):
    return v / (1.0 + jnp.exp(-v))


def activated(x, scale, shift):
    return silu(x * scale + shift)


def frame_taps(f, x_ref, left_ref, right_ref, scale, shift, pad_ref, out_ref):
    rows = x_ref.shape[1]
    _, col = tile_place()
    act = activated(x_ref[f].astype(F32), scale[None], shift[None])
    span = slice((2 + f) * rows, (3 + f) * rows)
    left = activated(left_ref[span], scale, shift)
    right = activated(right_ref[span], scale, shift)
    left = jnp.where(col > 0, left, 0.0)
    right = jnp.where(col < TCOL - 1, right, 0.0)
    pad_ref[...] = jnp.zeros_like(pad_ref)
    build_taps(act, left, right, pad_ref, out_ref, rows)


def finish_rows(total, x, bias, rows, width):
    chans = total.shape[-1]
    return (x.astype(F32) + bias[None] + total.reshape(rows, WP, chans)[:, :width]).astype(BF16)


def frame0_kernel(tiles, stat_ref, x_ref, left_ref, right_ref, v_ref, acc0_ref, gain_ref, bias_ref,
                  y_ref, coef_ref, xa_ref, pad_ref):
    _, rows, width, chans = x_ref.shape
    part = rows * width * (chans // GROUPS)
    count = part * tiles
    stat = stat_ref[...].reshape(tiles, 128)
    moved = pltpu.roll(stat, GROUPS, 1)
    mean = jnp.sum(stat, axis=0, keepdims=True) * (1.0 / count)
    mean_moved = jnp.sum(moved, axis=0, keepdims=True) * (1.0 / count)
    off = moved * (1.0 / part) - mean_moved
    var = jnp.sum(stat + part * off * off, axis=0, keepdims=True) * (1.0 / count)
    lane = lax.broadcasted_iota(jnp.int32, (1, 128), 1)
    is_mean = ((lane >> 5) & 1) == 0
    both = jnp.where(is_mean, mean, lax.rsqrt(jnp.maximum(var, 0.0) + EPS))
    both = jnp.broadcast_to(both, (8, 128))
    gain = gain_ref[...]
    for f in range(2):
        means = exact_dot(both, from_group(chans, 2 * f))[0:1]
        rstds = exact_dot(both, from_group(chans, 2 * f + 1))[0:1]
        scale = rstds * gain
        coef_ref[2 * f : 2 * f + 1, :] = scale
        coef_ref[2 * f + 1 : 2 * f + 2, :] = -means * scale
    frame_taps(0, x_ref, left_ref, right_ref, coef_ref[0:1], coef_ref[1:2], pad_ref, xa_ref)
    inner = rows - 2
    total = acc0_ref[...]
    for a in range(3):
        lhs = xa_ref[a : a + inner].reshape(inner * WP, 3 * chans)
        total = total + jnp.dot(lhs, v_ref[a, :, 0:chans], preferred_element_type=F32)
    y_ref[...] = finish_rows(total, x_ref[0, 1 : rows - 1], bias_ref[...], inner, width)


def frame1_kernel(x_ref, left_ref, right_ref, v_ref, acc1_ref, coef_ref, bias_ref, xa0_ref,
                  y_ref, xa_ref, pad_ref):
    _, rows, width, chans = x_ref.shape
    frame_taps(1, x_ref, left_ref, right_ref, coef_ref[2:3], coef_ref[3:4], pad_ref, xa_ref)
    inner = rows - 2
    total = acc1_ref[...]
    for a in range(3):
        lhs = xa0_ref[a : a + inner].reshape(inner * WP, 3 * chans)
        total = total + jnp.dot(lhs, v_ref[a, :, chans : 2 * chans], preferred_element_type=F32)
        lhs = xa_ref[a : a + inner].reshape(inner * WP, 3 * chans)
        total = total + jnp.dot(lhs, v_ref[a, :, 0:chans], preferred_element_type=F32)
    y_ref[...] = finish_rows(total, x_ref[1, 1 : rows - 1], bias_ref[...], inner, width)


def edge_kernel(x_ref, above_ref, below_ref, v_ref, coef_ref, bias_ref, x0_ref, x1_ref, xa0_ref, xa1_ref,
                y_ref, new_ref, pad_ref, halo_ref):
    _, rows, width, chans = x_ref.shape
    row, col = tile_place()
    last = lax.div(lax.axis_size("tile"), TCOL) - 1
    pad_ref[...] = jnp.zeros_like(pad_ref)
    total0 = jnp.zeros((2 * WP, chans), F32)
    total1 = jnp.zeros((2 * WP, chans), F32)
    for k, taps_ref in enumerate((x0_ref, x1_ref, xa0_ref, xa1_ref)):
        for side, src in ((0, above_ref), (1, below_ref)):
            cells = src[k].astype(F32)
            if k >= 2:
                f = k - 2
                cells = activated(cells, coef_ref[2 * f : 2 * f + 1], coef_ref[2 * f + 1 : 2 * f + 2])
                at = lax.broadcasted_iota(jnp.int32, cells.shape, 0)
                inside = (row > 0) if side == 0 else (row < last)
                keep = (at < width) | ((at == width) & (col > 0)) | ((at == width + 1) & (col < TCOL - 1))
                cells = jnp.where(keep & inside, cells, 0.0)
            pad_ref[side, 8 : 8 + width, :] = cells[0:width]
            pad_ref[side, 7:8, :] = cells[width : width + 1]
            pad_ref[side, 8 + width : 9 + width, :] = cells[width + 1 : width + 2]
        for b in range(3):
            halo_ref[:, :, b * chans : (b + 1) * chans] = pad_ref[0:2, 7 + b : 7 + b + WP, :].astype(BF16)
        lo, hi = ((2, 3), (1, 3), (0, 2), (0, 1))[k]
        for a in range(3):
            up = halo_ref[0] if a == 0 else taps_ref[a - 1]
            down = halo_ref[1] if a == 2 else taps_ref[rows - 2 + a]
            lhs = jnp.concatenate([up, down], axis=0)
            part = jnp.dot(lhs, v_ref[a, :, lo * chans : hi * chans], preferred_element_type=F32)
            if k == 0:
                total0 = total0 + part
            elif k == 3:
                total1 = total1 + part
            else:
                total0 = total0 + part[:, :chans]
                total1 = total1 + part[:, chans:]
    for f, total in ((0, total0), (1, total1)):
        for side, r in ((0, 0), (1, rows - 1)):
            y_ref[f, side] = (x_ref[f, r].astype(F32) + bias_ref[...]
                              + total[side * WP : side * WP + width]).astype(BF16)
    new_ref[0] = xa0_ref[:, 0:width, chans : 2 * chans]
    new_ref[1] = xa1_ref[:, 0:width, chans : 2 * chans]


def join_kernel(y0_ref, y1_ref, edge_ref, out_ref, sems):
    rows = out_ref.shape[1]
    copies = []
    for f, src in ((0, y0_ref), (1, y1_ref)):
        copies.append(pltpu.make_async_copy(src, out_ref.at[f, 1 : rows - 1], sems.at[f, 0]))
        copies.append(pltpu.make_async_copy(edge_ref.at[f, 0], out_ref.at[f, 0], sems.at[f, 1]))
        copies.append(pltpu.make_async_copy(edge_ref.at[f, 1], out_ref.at[f, rows - 1], sems.at[f, 2]))
    for copy in copies:
        copy.start()
    for copy in copies:
        copy.wait()


def on_device(frames_in, cache, kernel, gain, conv_bias):
    x = frames_in[0][:, 0]
    c = cache[0][:, 0]
    frames, rows, width, chans = x.shape
    tiles = lax.axis_size("tile")
    sections = lax.axis_size("section")
    weights = kernel.reshape(3, 3, 3 * chans, chans)
    inner = rows - 2
    sds = jax.ShapeDtypeStruct

    stat, send_a, send_b = pl.pallas_call(
        first_kernel,
        out_shape=(sds((tiles, 1, 128), F32), sds((4 * rows, chans), BF16), sds((4 * rows, chans), BF16)),
        in_specs=[VMEM] * 2, out_specs=[VMEM] * 3,
        scratch_shapes=[pltpu.VMEM((4 * rows, chans), F32)] * 2,
        compiler_params=params(), name="local_stats",
    )(x, c)
    swap_a = [(i, i ^ 1) for i in range(tiles)]
    swap_b = [(i, i + (1 if i % 2 else -1)) for i in range(tiles) if i % TCOL in (1, 2)]
    recv_a = lax.ppermute(send_a, "tile", swap_a)
    recv_b = lax.ppermute(send_b, "tile", swap_b)
    stats = lax.all_to_all(stat, "tile", 0, 0, tiled=True)

    taps = pltpu.VMEM((rows, WP, 3 * chans), BF16)
    acc = pltpu.VMEM((inner * WP, chans), F32)
    cols = pltpu.VMEM((4 * rows, chans), F32)
    v, x0, x1, acc0, acc1, top, bottom, left, right = pl.pallas_call(
        cache_kernel,
        out_shape=(pltpu.VMEM((3, 3 * chans, 3 * chans), BF16), taps, taps, acc, acc,
                   sds((4, WP, chans), BF16), sds((4, WP, chans), BF16), cols, cols),
        in_specs=[VMEM] * 4 + [ANY], out_specs=[VMEM] * 9,
        scratch_shapes=[pltpu.VMEM((rows, 80, chans), F32), pltpu.VMEM((WP, chans), F32),
                        pltpu.SemaphoreType.DMA((3, 3))],
        compiler_params=params(), name="cache_part",
    )(c, x, recv_a, recv_b, weights)
    above = lax.ppermute(bottom, "tile", [(i, i + TCOL) for i in range(tiles - TCOL)])
    below = lax.ppermute(top, "tile", [(i + TCOL, i) for i in range(tiles - TCOL)])

    onward = [(i, (i + 1) % sections) for i in range(sections)]
    y0, coef, xa0 = pl.pallas_call(
        functools.partial(frame0_kernel, tiles),
        out_shape=(sds((inner, width, chans), BF16), pltpu.VMEM((8, chans), F32), taps),
        in_specs=[VMEM] * 8, out_specs=[VMEM] * 3,
        scratch_shapes=[pltpu.VMEM((rows, 80, chans), F32)],
        compiler_params=params(), name="frame0_inner",
    )(stats, x, left, right, v, acc0, gain, conv_bias)
    y0 = lax.ppermute(y0, "section", onward)
    y1, xa1 = pl.pallas_call(
        frame1_kernel,
        out_shape=(sds((inner, width, chans), BF16), taps),
        in_specs=[VMEM] * 8, out_specs=[VMEM] * 2,
        scratch_shapes=[pltpu.VMEM((rows, 80, chans), F32)],
        compiler_params=params(), name="frame1_inner",
    )(x, left, right, v, acc1, coef, conv_bias, xa0)
    y1 = lax.ppermute(y1, "section", onward)
    edge, new = pl.pallas_call(
        edge_kernel,
        out_shape=(sds((2, 2, width, chans), BF16), sds((frames, rows, width, chans), BF16)),
        in_specs=[VMEM] * 10, out_specs=[VMEM] * 2,
        scratch_shapes=[pltpu.VMEM((2, 80, chans), F32), pltpu.VMEM((2, WP, 3 * chans), BF16)],
        compiler_params=params(), name="edge_rows",
    )(x, above, below, v, coef, conv_bias, x0, x1, xa0, xa1)
    edge = lax.ppermute(edge, "section", onward)
    handed = pl.pallas_call(
        join_kernel,
        out_shape=sds((frames, rows, width, chans), BF16),
        in_specs=[ANY] * 3, out_specs=ANY,
        scratch_shapes=[pltpu.SemaphoreType.DMA((2, 3))],
        compiler_params=params(), name="join_rows",
    )(y0, y1, edge)
    return (handed[None, :, None], new[None, :, None])


def solution(mesh):
    tiled = P("section", None, "tile", None, None, None)
    in_specs = (tiled, tiled, P("section", None, None, None, None, None), P("section", None), P("section", None))
    return jax.shard_map(
        on_device, mesh=mesh, in_specs=in_specs, out_specs=(tiled, tiled), check_vma=False
    )
```

time: 254 us -> 68.3 us (0.27)
  blocking collectives: 131 us -> 15 us
  local copies, waits for them, and re-layouts: 46.7 us -> 7.49 us
  other arithmetic: 24.7 us -> 0 us
  matrix products: 20.8 us -> 0 us
  Pallas kernels: 0 us -> 16.3 us
  waiting for transfers between devices: 19 us -> 13.8 us
  starting transfers between devices: 10.1 us -> 14.8 us
    psum x2 -> x0, blocking collectives: 131 us -> none  [the longest x1 65.6 us: on_device(): lax.psum(jnp.sum(deviation * deviation, axis=(1, 2, 4)), 'tile') / count]
    reshape x9 -> x0, local copies, waits for them, and re-layouts: 22 us -> none  [the longest x8 20.6 us: convolve(): taps = taps.reshape(-1, 3 * chans)]
    dot_general x9 -> x0, matrix products: 20.8 us -> none  [convolve(): total = total + jnp.dot(taps, matrix, preferred_element_type=jnp.float32)]
    concatenate x10 -> x0, other arithmetic: 20.4 us -> none  [the longest x7 13.6 us: convolve(): jnp.concatenate([block[:, :, step_w:step_w + width] for step_w in range(3...]
    pallas_call x0 -> x6, Pallas kernels: none -> 16.3 us  [the longest x1 7.07 us: on_device(): pl.pallas_call(cache_kernel, out_shape=(pltpu.VMEM((3, 3 * chans, 3 * cha...]
    all_to_all x0 -> x1, blocking collectives: none -> 15 us  [on_device(): stats = lax.all_to_all(stat, 'tile', 0, 0, tiled=True)]
    slice x3 -> x0, local copies, waits for them, and re-layouts: 13.4 us -> none  [the longest x2 7.73 us: convolve(): block[:, :, step_w:step_w + width]]
    ppermute x5 -> x7, waiting for transfers between devices: 19 us -> 13.8 us  [the longest x1 6.32 us: on_device(): y1 = lax.ppermute(y1, 'section', onward)]
  transfers between devices with their start and end apart: 5 -> 7, of which waited for: 1 -> 3; matrix products, arithmetic and copies ran while one was open for 14% -> 2% of each run, Pallas kernels for 0% -> 12%
where the time goes in v1:
time: 68.3 us; the launch traced here: 68.1 us
  Pallas kernels  16.3 us (24%)
  blocking collectives  15 us (22%)
  starting transfers between devices  14.8 us (22%)
  waiting for transfers between devices  13.8 us (20%)
  local copies, waits for them, and re-layouts  7.49 us (11%)
  between operations  0.72 us (1%)
    all_to_all x1, blocking collectives, on_device(): stats = lax.all_to_all(stat, 'tile', 0, 0, tiled=True)  15 us
    pallas_call x1, Pallas kernels, on_device(): pl.pallas_call(cache_kernel, out_shape=(pltpu.VMEM((3, 3 * chans, 3 * cha...  7.07 us
    ppermute x1, waiting for transfers between devices, on_device(): y1 = lax.ppermute(y1, 'section', onward)  6.32 us
    unnamed x8, local copies, waits for them, and re-layouts  5.86 us
    ppermute x1, waiting for transfers between devices, on_device(): edge = lax.ppermute(edge, 'section', onward)  4.21 us
    ppermute x1, starting transfers between devices, on_device(): recv_a = lax.ppermute(send_a, 'tile', swap_a)  3.33 us
    ppermute x1, waiting for transfers between devices, on_device(): recv_b = lax.ppermute(send_b, 'tile', swap_b)  3.21 us
    pallas_call x1, Pallas kernels, on_device(): pl.pallas_call(frame1_kernel, out_shape=(sds((inner, width, chans), BF16)...  3.19 us
  transfers between devices with their start and end apart: 7, of which 3 were waited for; matrix products, arithmetic and copies ran while one was open for 2% of the time, Pallas kernels for 12%

profile of v1, /device:TPU:1, one launch (start us, length us, event | category | flops | bytes accessed | tf_op | source)
XLA Modules:
  0.0 68.1 jit_solution(4460968258680648622)
XLA Ops:
  0.6 1.6 %copy_bitcast_fusion = (bf16[2,8,60,384]{3,2,1,0:T(8,128)(2,1)S(1)}, bf16[2,8,60,384]{3,2,1,0:T(8,128)(2,1)S(1)}) fusion(bf16[1,2,1,8,60,384]{5,3,4,2,1,0:T(8,128)(2,1)} %param.6, bf16[1,2,1,8,60,384]{5,3,4,2,1,0:T(8,128)(2,1)} %param.5), kind=kLoop, calls=%fused_computation | loop fusion | bytes 2949120 | tf_op jit(solution)/shard_map/squeeze;squeeze | solution.py:293
  2.3 0.8 %local_stats.1 = (f32[32,1,128]{2,1,0:T(1,128)S(1)}, bf16[32,384]{1,0:T(8,128)(2,1)S(1)}, bf16[32,384]{1,0:T(8,128)(2,1)S(1)}) custom-call(bf16[2,8,60,384]{3,2,1,0:T(8,128)(2,1)S(1)} %get-tuple-element.43.x_ref, bf16[2,8,60,384]{3,2,1,0:T(8,128)(2,1)S(1)} %get-tuple-element.42.c_ref), custom_call_target="tpu_custom_call" | custom-call | tf_op jit(solution)/shard_map/local_stats/pallas_call | solution.py:301
  3.1 3.3 %collective-permute-start = (bf16[32,384]{1,0:T(8,128)(2,1)S(1)}, bf16[32,384]{1,0:T(8,128)(2,1)S(1)}, u32[]{:S(2)}, u32[]{:S(2)}) collective-permute-start(bf16[32,384]{1,0:T(8,128)(2,1)S(1)} %get-tuple-element.22), channel_id=1, source_target_pairs={{0,1},{1,0},{2,3},{3,2},{4,5},{5,4},{6,7},{7,6},{8,9},{9,8},{10,11... | collective-permute-start | bytes 73736 | tf_op jit(solution)/shard_map/ppermute | solution.py:310
  6.4 1.9 %collective-permute-start.1 = (bf16[32,384]{1,0:T(8,128)(2,1)S(1)}, bf16[32,384]{1,0:T(8,128)(2,1)S(1)}, u32[]{:S(2)}, u32[]{:S(2)}) collective-permute-start(bf16[32,384]{1,0:T(8,128)(2,1)S(1)} %get-tuple-element.23), channel_id=1, source_target_pairs={{1,2},{2,1},{5,6},{6,5},{9,10},{10,9},{13,14},{14,13},{17,18},{18,... | collective-permute-start | bytes 73736 | tf_op jit(solution)/shard_map/ppermute | solution.py:311
  8.3 0.0 collective-permute-done.recv_a_ref
  8.3 3.2 %collective-permute-done.1.recv_b_ref = bf16[32,384]{1,0:T(8,128)(2,1)S(1)} collective-permute-done((bf16[32,384]{1,0:T(8,128)(2,1)S(1)}, bf16[32,384]{1,0:T(8,128)(2,1)S(1)}, u32[]{:S(2)}, u32[]{:S(2)}) %collective-permute-start.1) | collective-permute-done | bytes 24608 | tf_op jit(solution)/shard_map/ppermute | solution.py:311
  11.5 0.0 copy-start
  11.5 3.3 %copy-done = bf16[1,3,3,3,384,384]{5,4,3,2,1,0:T(8,128)(2,1)S(1)} copy-done((bf16[1,3,3,3,384,384]{5,4,3,2,1,0:T(8,128)(2,1)S(1)}, bf16[1,3,3,3,384,384]{5,4,3,2,1,0:T(8,128)(2,1)}, u32[]{:S(2)}) %copy-start) | copy-done | bytes 7962648
  14.8 0.0 copy-start.1
  14.8 0.0 copy-start.2
  14.8 7.1 %cache_part.1 = (bf16[3,1152,1152]{2,1,0:T(8,128)(2,1)S(1)}, bf16[8,64,1152]{2,1,0:T(8,128)(2,1)S(1)}, bf16[8,64,1152]{2,1,0:T(8,128)(2,1)S(1)}, f32[384,384]{1,...) custom-call(bf16[2,8,60,384]{3,2,1,0:T(8,128)(2,1)S(1)} %get-tuple-e, ...), custom_call_target="tpu_custom_call" | custom-call | tf_op jit(solution)/shard_map/cache_part/pallas_call | solution.py:317
  21.9 2.9 %collective-permute-start.4 = (bf16[4,64,384]{2,1,0:T(8,128)(2,1)S(1)}, bf16[4,64,384]{2,1,0:T(8,128)(2,1)S(1)}, u32[]{:S(2)}, u32[]{:S(2)}) collective-permute-start(bf16[4,64,384]{2,1,0:T(8,128)(2,1)S(1)} %get-tuple-element.33), channel_id=1, source_target_pairs={{0,4},{1,5},{2,6},{3,7},{4,8},{5,9},{6,10},{7,11},{8,12},{9,13},{1... | collective-permute-start | bytes 589832 | tf_op jit(solution)/shard_map/ppermute | solution.py:326
  24.8 1.3 %collective-permute-start.5 = (bf16[4,64,384]{2,1,0:T(8,128)(2,1)S(1)}, bf16[4,64,384]{2,1,0:T(8,128)(2,1)S(1)}, u32[]{:S(2)}, u32[]{:S(2)}) collective-permute-start(bf16[4,64,384]{2,1,0:T(8,128)(2,1)S(1)} %get-tuple-element.34), channel_id=1, source_target_pairs={{4,0},{5,1},{6,2},{7,3},{8,4},{9,5},{10,6},{11,7},{12,8},{13,9},{1... | collective-permute-start | bytes 589832 | tf_op jit(solution)/shard_map/ppermute | solution.py:327
  26.1 15.0 %all_to_all.5.stat_ref = f32[32,1,128]{2,1,0:T(1,128)S(1)} all-to-all(f32[32,1,128]{2,1,0:T(1,128)S(1)} %get-tuple-element.21), channel_id=1, replica_groups=mesh['section'=8,'tile'=32] {'tile'}, dimensions={0} | all-to-all | bytes 32768 | tf_op jit(solution)/shard_map/all_to_all | solution.py:312
  41.1 0.0 copy-done.1
  41.1 0.0 copy-done.2
  41.1 2.1 %frame0_inner.1 = (bf16[6,60,384]{2,1,0:T(8,128)(2,1)S(1)}, f32[8,384]{1,0:T(8,128)S(1)}, bf16[8,64,1152]{2,1,0:T(8,128)(2,1)S(1)}) custom-call(f32[32,1,128]{2,1,0:T(1,128)S(1)} %all_to_all.5.stat_ref, bf16[2,8,60,384]{3,2,1,0:T(8,128)(2,1)S(1)} %get-tuple-element.43.x_ref, f32[32,384]{1,0:T(8,128)S(1)} %get-tuple-element.24.left_ref, ...), custom_call_target="tpu_custom_call" | custom-call | tf_op jit(solution)/shard_map/frame0_inner/pallas_call | solution.py:330
  43.2 1.9 %collective-permute-start.2 = (bf16[6,60,384]{2,1,0:T(8,128)(2,1)S(1)}, bf16[6,60,384]{2,1,0:T(8,128)(2,1)S(1)}, u32[]{:S(2)}, u32[]{:S(2)}) collective-permute-start(bf16[6,60,384]{2,1,0:T(8,128)(2,1)S(1)} %get-tuple-element.28), channel_id=1, source_target_pairs={{0,32},{32,64},{64,96},{96,128},{128,160},{160,192},{192,224},{224... | collective-permute-start | bytes 829448 | tf_op jit(solution)/shard_map/ppermute | solution.py:337
  45.1 3.2 %frame1_inner.1 = (bf16[6,60,384]{2,1,0:T(8,128)(2,1)S(1)}, bf16[8,64,1152]{2,1,0:T(8,128)(2,1)S(1)}) custom-call(bf16[2,8,60,384]{3,2,1,0:T(8,128)(2,1)S(1)} %get-tuple-element.43.x_ref, f32[32,384]{1,0:T(8,128)S(1)} %get-tuple-element.24.left_ref, f32[32,384]{1,0:T(8,128)S(1)} %get-tuple-element.25.right_ref, ...), custom_call_target="tpu_custom_call" | custom-call | tf_op jit(solution)/shard_map/frame1_inner/pallas_call | solution.py:338
  48.3 1.7 %collective-permute-start.3 = (bf16[6,60,384]{2,1,0:T(8,128)(2,1)S(1)}, bf16[6,60,384]{2,1,0:T(8,128)(2,1)S(1)}, u32[]{:S(2)}, u32[]{:S(2)}) collective-permute-start(bf16[6,60,384]{2,1,0:T(8,128)(2,1)S(1)} %get-tuple-element.32), channel_id=1, source_target_pairs={{0,32},{32,64},{64,96},{96,128},{128,160},{160,192},{192,224},{224... | collective-permute-start | bytes 829448 | tf_op jit(solution)/shard_map/ppermute | solution.py:345
  50.0 0.0 collective-permute-done.4.above_ref
  50.0 0.0 collective-permute-done.5.below_ref
  50.0 2.7 %edge_rows.1 = (bf16[2,2,60,384]{3,2,1,0:T(8,128)(2,1)S(1)}, bf16[2,8,60,384]{3,2,1,0:T(8,128)(2,1)S(1)}) custom-call(bf16[2,8,60,384]{3,2,1,0:T(8,128)(2,1)S(1)} %get-tuple-element.43.x_ref, bf16[4,64,384]{2,1,0:T(8,128)(2,1)S(1)} %collective-permute-done.4.above_ref, bf16[4,64,384]{2,1,0:T(8,128)(2,1)S(1)} %collective-permute-done.5.below_ref, ...), custom_call_target="tpu_custom_call" | custom-call | tf_op jit(solution)/shard_map/edge_rows/pallas_call | solution.py:346
  52.8 1.7 %collective-permute-start.6 = (bf16[2,2,60,384]{3,2,1,0:T(8,128)(2,1)S(1)}, bf16[2,2,60,384]{3,2,1,0:T(8,128)(2,1)S(1)}, u32[]{:S(2)}, u32[]{:S(2)}) collective-permute-start(bf16[2,2,60,384]{3,2,1,0:T(8,128)(2,1)S(1)} %get-tuple-element.38), channel_id=1, source_target_pairs={{0,32},{32,64},{64,96},{96,128},{128,160},{160,192},{192,224},{224... | collective-permute-start | bytes 552968 | tf_op jit(solution)/shard_map/ppermute | solution.py:353
  54.5 1.3 %copy.10 = bf16[1,2,1,8,60,384]{5,3,4,2,1,0:T(8,128)(2,1)} copy(bf16[1,2,1,8,60,384]{5,4,3,1,2,0:T(8,128)(2,1)S(1)} %bitcast.9) | data formatting | bytes 1474560
  55.8 0.0 collective-permute-done.2.y0_ref
  55.8 6.3 %collective-permute-done.3.y1_ref = bf16[6,60,384]{2,1,0:T(8,128)(2,1)S(1)} collective-permute-done((bf16[6,60,384]{2,1,0:T(8,128)(2,1)S(1)}, bf16[6,60,384]{2,1,0:T(8,128)(2,1)S(1)}, u32[]{:S(2)}, u32[]{:S(2)}) %collective-permute-start.3) | collective-permute-done | bytes 276512 | tf_op jit(solution)/shard_map/ppermute | solution.py:345
  62.1 4.2 %collective-permute-done.6.edge_ref = bf16[2,2,60,384]{3,2,1,0:T(8,128)(2,1)S(1)} collective-permute-done((bf16[2,2,60,384]{3,2,1,0:T(8,128)(2,1)S(1)}, bf16[2,2,60,384]{3,2,1,0:T(8,128)(2,1)S(1)}, u32[]{:S(2)}, u32[]{:S(2)}) %collective-permute-start.6) | collective-permute-done | bytes 184352 | tf_op jit(solution)/shard_map/ppermute | solution.py:353
  66.3 0.4 join_rows.1
  66.8 1.3 %copy.9 = bf16[1,2,1,8,60,384]{5,3,4,2,1,0:T(8,128)(2,1)} copy(bf16[1,2,1,8,60,384]{5,4,3,1,2,0:T(8,128)(2,1)S(1)} %bitcast.8) | data formatting | bytes 1474560
Async XLA Ops:
  3.1 5.2 %collective-permute-start = (bf16[32,384]{1,0:T(8,128)(2,1)S(1)}, bf16[32,384]{1,0:T(8,128)(2,1)S(1)}, u32[]{:S(2)}, u32[]{:S(2)}) collective-permute-start(bf16[32,384]{1,0:T(8,128)(2,1)S(1)} %get-tuple-element.22), channel_id=1, source_target_pairs={{0,1},{1,0},{2,3},{3,2},{4,5},{5,4},{6,7},{7,6},{8,9},{9,8},{10,11... | collective-permute-start | bytes 73736 | tf_op jit(solution)/shard_map/ppermute | solution.py:310
  6.4 5.1 %collective-permute-start.1 = (bf16[32,384]{1,0:T(8,128)(2,1)S(1)}, bf16[32,384]{1,0:T(8,128)(2,1)S(1)}, u32[]{:S(2)}, u32[]{:S(2)}) collective-permute-start(bf16[32,384]{1,0:T(8,128)(2,1)S(1)} %get-tuple-element.23), channel_id=1, source_target_pairs={{1,2},{2,1},{5,6},{6,5},{9,10},{10,9},{13,14},{14,13},{17,18},{18,... | collective-permute-start | bytes 73736 | tf_op jit(solution)/shard_map/ppermute | solution.py:311
  11.5 3.3 %copy-start = (bf16[1,3,3,3,384,384]{5,4,3,2,1,0:T(8,128)(2,1)S(1)}, bf16[1,3,3,3,384,384]{5,4,3,2,1,0:T(8,128)(2,1)}, u32[]{:S(2)}) copy-start(bf16[1,3,3,3,384,384]{5,4,3,2,1,0:T(8,128)(2,1)} %param.7) | copy-start | bytes 23887876
  14.8 26.3 %copy-start.1 = (f32[1,384]{1,0:T(1,128)S(1)}, f32[1,384]{1,0:T(1,128)}, u32[]{:S(2)}) copy-start(f32[1,384]{1,0:T(1,128)} %bias_ref.5) | copy-start | bytes 4612
  14.8 26.3 %copy-start.2 = (f32[1,384]{1,0:T(1,128)S(1)}, f32[1,384]{1,0:T(1,128)}, u32[]{:S(2)}) copy-start(f32[1,384]{1,0:T(1,128)} %gain_ref.1) | copy-start | bytes 4612
  21.9 28.2 %collective-permute-start.4 = (bf16[4,64,384]{2,1,0:T(8,128)(2,1)S(1)}, bf16[4,64,384]{2,1,0:T(8,128)(2,1)S(1)}, u32[]{:S(2)}, u32[]{:S(2)}) collective-permute-start(bf16[4,64,384]{2,1,0:T(8,128)(2,1)S(1)} %get-tuple-element.33), channel_id=1, source_target_pairs={{0,4},{1,5},{2,6},{3,7},{4,8},{5,9},{6,10},{7,11},{8,12},{9,13},{1... | collective-permute-start | bytes 589832 | tf_op jit(solution)/shard_map/ppermute | solution.py:326
  24.8 25.2 %collective-permute-start.5 = (bf16[4,64,384]{2,1,0:T(8,128)(2,1)S(1)}, bf16[4,64,384]{2,1,0:T(8,128)(2,1)S(1)}, u32[]{:S(2)}, u32[]{:S(2)}) collective-permute-start(bf16[4,64,384]{2,1,0:T(8,128)(2,1)S(1)} %get-tuple-element.34), channel_id=1, source_target_pairs={{4,0},{5,1},{6,2},{7,3},{8,4},{9,5},{10,6},{11,7},{12,8},{13,9},{1... | collective-permute-start | bytes 589832 | tf_op jit(solution)/shard_map/ppermute | solution.py:327
  43.2 12.6 %collective-permute-start.2 = (bf16[6,60,384]{2,1,0:T(8,128)(2,1)S(1)}, bf16[6,60,384]{2,1,0:T(8,128)(2,1)S(1)}, u32[]{:S(2)}, u32[]{:S(2)}) collective-permute-start(bf16[6,60,384]{2,1,0:T(8,128)(2,1)S(1)} %get-tuple-element.28), channel_id=1, source_target_pairs={{0,32},{32,64},{64,96},{96,128},{128,160},{160,192},{192,224},{224... | collective-permute-start | bytes 829448 | tf_op jit(solution)/shard_map/ppermute | solution.py:337
  48.3 13.8 %collective-permute-start.3 = (bf16[6,60,384]{2,1,0:T(8,128)(2,1)S(1)}, bf16[6,60,384]{2,1,0:T(8,128)(2,1)S(1)}, u32[]{:S(2)}, u32[]{:S(2)}) collective-permute-start(bf16[6,60,384]{2,1,0:T(8,128)(2,1)S(1)} %get-tuple-element.32), channel_id=1, source_target_pairs={{0,32},{32,64},{64,96},{96,128},{128,160},{160,192},{192,224},{224... | collective-permute-start | bytes 829448 | tf_op jit(solution)/shard_map/ppermute | solution.py:345
  52.8 13.6 %collective-permute-start.6 = (bf16[2,2,60,384]{3,2,1,0:T(8,128)(2,1)S(1)}, bf16[2,2,60,384]{3,2,1,0:T(8,128)(2,1)S(1)}, u32[]{:S(2)}, u32[]{:S(2)}) collective-permute-start(bf16[2,2,60,384]{3,2,1,0:T(8,128)(2,1)S(1)} %get-tuple-element.38), channel_id=1, source_target_pairs={{0,32},{32,64},{64,96},{96,128},{128,160},{160,192},{192,224},{224... | collective-permute-start | bytes 552968 | tf_op jit(solution)/shard_map/ppermute | solution.py:353

commit v2 on v0

v2 whole, which is shorter than its diff:
```python
import functools

import jax
import jax.numpy as jnp
from jax import lax
from jax.experimental import pallas as pl
from jax.experimental.pallas import tpu as pltpu
from jax.sharding import PartitionSpec as P

GROUPS = 32
TCOL = 4
EPS = 1e-06
WP = 64
F32 = jnp.float32
BF16 = jnp.bfloat16
VMEM = pl.BlockSpec(memory_space=pltpu.VMEM)
ANY = pl.BlockSpec(memory_space=pl.ANY)
LIMIT = 20 * 1024 * 1024


def cost(us):
    return pl.CostEstimate(flops=int(us * 1e9), bytes_accessed=int(us * 3e6), transcendentals=0)


def params():
    return pltpu.CompilerParams(vmem_limit_bytes=LIMIT)


def split3(x):
    high = x.astype(BF16)
    rest = x - high.astype(F32)
    mid = rest.astype(BF16)
    low = (rest - mid.astype(F32)).astype(BF16)
    return high, mid, low


def exact_dot(x, onehot):
    pad = jnp.zeros_like(x)
    parts = split3(x)
    lhs = jnp.concatenate([jnp.concatenate([p.astype(F32), pad], axis=0) for p in parts], axis=0)
    got = jnp.dot(lhs.astype(BF16), onehot, preferred_element_type=F32)
    return got[0:8] + got[16:24] + got[32:40]


def to_group(chans, block):
    size = chans // GROUPS
    chan = lax.broadcasted_iota(jnp.int32, (chans, 128), 0)
    lane = lax.broadcasted_iota(jnp.int32, (chans, 128), 1)
    first = (lane & (GROUPS - 1)) * size
    hit = (chan >= first) & (chan < first + size)
    if block is not None:
        hit = hit & ((lane >> 5) == block)
    return jnp.where(hit, 1.0, 0.0).astype(BF16)


def from_group(chans, block):
    size = chans // GROUPS
    lane = lax.broadcasted_iota(jnp.int32, (128, chans), 0)
    chan = lax.broadcasted_iota(jnp.int32, (128, chans), 1)
    first = (lane & (GROUPS - 1)) * size
    hit = (chan >= first) & (chan < first + size) & ((lane >> 5) == block)
    return jnp.where(hit, 1.0, 0.0).astype(BF16)


PARTS = 4


def fetch(hbm_ref, f, vmem_ref, sems):
    step = hbm_ref.shape[1] // PARTS
    copies = [pltpu.make_async_copy(hbm_ref.at[f, pl.ds(p * step, step)], vmem_ref.at[pl.ds(p * step, step)],
                                    sems.at[p]) for p in range(PARTS)]
    for copy in copies:
        copy.start()
    return copies


def wait_all(copies):
    for copy in copies:
        copy.wait()


def first_kernel(x_hbm, c_hbm, stat_ref, first_ref, last_ref, x_ref, edge_ref, sems, edge_sems):
    frames, width, rows, chans = x_ref.shape
    loads = [fetch(x_hbm, f, x_ref.at[f], sems.at[f]) for f in range(frames)]
    edges = []
    for f in range(2):
        for at, w in ((0, 0), (1, width - 1)):
            edges.append(pltpu.make_async_copy(c_hbm.at[f, w], edge_ref.at[f, at], edge_sems.at[f, at]))
    for copy in edges:
        copy.start()
    size = chans // GROUPS
    count = rows * width
    sums, squares = [], []
    for f in range(frames):
        wait_all(loads[f])
        x = x_ref[f].astype(F32)
        total = jnp.sum(jnp.sum(x, axis=0), axis=0, keepdims=True)
        dev = x - (total * (1.0 / count))[None]
        sums.append(total)
        squares.append(jnp.sum(jnp.sum(dev * dev, axis=0), axis=0, keepdims=True))
    wait_all(edges)
    for k in range(4):
        first_ref[k] = edge_ref[k, 0] if k < 2 else x_ref[k - 2, 0]
        last_ref[k] = edge_ref[k, 1] if k < 2 else x_ref[k - 2, width - 1]
    zero = jnp.zeros((1, chans), F32)
    both = jnp.concatenate(sums + [zero] * 6, axis=0)
    grouped = exact_dot(both, to_group(chans, 0))
    spread = exact_dot(grouped, from_group(chans, 0))
    off = both * (1.0 / count) - spread * (1.0 / (count * size))
    square = jnp.concatenate(squares + [zero] * 6, axis=0) + count * off * off
    row = lax.broadcasted_iota(jnp.int32, (8, 128), 0)
    lane = lax.broadcasted_iota(jnp.int32, (8, 128), 1)
    every = to_group(chans, None)
    mix_sum = exact_dot(both, every)
    mix_square = exact_dot(square, every)
    kind = lane >> 5
    mixed = jnp.where((row == 0) & (kind == 0), mix_sum, 0.0)
    mixed = mixed + jnp.where((row == 1) & (kind == 2), mix_sum, 0.0)
    mixed = mixed + jnp.where((row == 0) & (kind == 1), mix_square, 0.0)
    mixed = mixed + jnp.where((row == 1) & (kind == 3), mix_square, 0.0)
    line = jnp.sum(mixed, axis=0, keepdims=True)
    stat_ref[...] = jnp.broadcast_to(line[None], stat_ref.shape)


LANES = 128


def put_lines(flat_ref, lines):
    for j in range(flat_ref.shape[0]):
        flat_ref[j] = lines[:, j * LANES : (j + 1) * LANES]


def get_row(flat_ref, r, rows, width):
    return jnp.concatenate(
        [flat_ref[j, pl.ds(r, width, stride=rows), :] for j in range(flat_ref.shape[0])], axis=1)


def put_row(flat_ref, r, rows, width, value):
    for j in range(flat_ref.shape[0]):
        flat_ref[j, pl.ds(r, width, stride=rows), :] = value[:, j * LANES : (j + 1) * LANES]


def build_taps(flat_ref, left, right, pad_ref, out_ref, rows, width):
    chans = pad_ref.shape[-1]
    for r in range(rows):
        pad_ref[r, 8 : 8 + width, :] = get_row(flat_ref, r, rows, width)
        pad_ref[r, 7:8, :] = left[r : r + 1]
        pad_ref[r, 8 + width : 9 + width, :] = right[r : r + 1]
    for b in range(3):
        out_ref[1 : 1 + rows, :, b * chans : (b + 1) * chans] = pad_ref[:, 7 + b : 7 + b + WP, :].astype(BF16)
    out_ref[0] = jnp.zeros_like(out_ref[0])
    out_ref[rows + 1] = jnp.zeros_like(out_ref[0])


def clear_tail(pad_ref, width):
    pad_ref[:, 8 + width :, :] = jnp.zeros_like(pad_ref[:, 8 + width :, :])


def tile_place():
    tile = lax.axis_index("tile")
    return lax.div(tile, TCOL), lax.rem(tile, TCOL)


BLOCK = 4


def wide_taps(taps_ref, first):
    return jnp.concatenate([taps_ref[first + a : first + a + BLOCK].reshape(BLOCK * WP, -1) for a in range(3)], axis=1)


def product(taps_ref, first, v_ref, at):
    return jnp.dot(wide_taps(taps_ref, first), tap_weights(v_ref, at, at + 1), preferred_element_type=F32)


def tap_weights(v_ref, lo, hi):
    chans = v_ref.shape[1] // 3
    return v_ref[:, :, lo * chans : hi * chans].reshape(9 * chans, (hi - lo) * chans)


def rows_kernel(c_hbm, x_hbm, from_left_ref, from_right_ref, bottom_ref, top_ref, left_ref, right_ref,
                frame_ref, flat_ref, sems):
    _, width, rows, chans = frame_ref.shape
    loads = [fetch(c_hbm if k < 2 else x_hbm, k % 2, frame_ref.at[k], sems.at[k]) for k in range(4)]
    _, col = tile_place()
    left_ref[...] = jnp.where(col > 0, from_left_ref[...].astype(F32), 0.0)
    right_ref[...] = jnp.where(col < TCOL - 1, from_right_ref[...].astype(F32), 0.0)
    for k in range(4):
        wait_all(loads[k])
        put_lines(flat_ref, frame_ref[k].astype(F32).reshape(width * rows, chans))
        for out_ref, r in ((bottom_ref, rows - 1), (top_ref, 0)):
            last = jnp.concatenate([left_ref[k, r : r + 1], right_ref[k, r : r + 1],
                                    jnp.zeros((WP - width - 2, chans), F32)], axis=0)
            line = jnp.concatenate([get_row(flat_ref, r, rows, width), last], axis=0)
            out_ref[k] = line.astype(BF16)


def silu(v):
    return v / (1.0 + jnp.exp(-v))


def activated(x, scale, shift):
    return silu(x * scale + shift)


def frame_taps(f, x_ref, left_ref, right_ref, scale, shift, pad_ref, flat_ref, new_ref, out_ref):
    _, width, rows, chans = x_ref.shape
    _, col = tile_place()
    act = activated(x_ref[f].astype(F32).reshape(width * rows, chans), scale, shift)
    put_lines(flat_ref, act)
    new_ref[...] = act.astype(BF16).reshape(width, rows, chans)
    left = activated(left_ref[2 + f], scale, shift)
    right = activated(right_ref[2 + f], scale, shift)
    left = jnp.where(col > 0, left, 0.0)
    right = jnp.where(col < TCOL - 1, right, 0.0)
    clear_tail(pad_ref, width)
    build_taps(flat_ref, left, right, pad_ref, out_ref, rows, width)


def finish_rows(total, first, flat_ref, bias, width, rows, y_ref, rim_ref, skip=0):
    for at in range(BLOCK):
        r = first + at
        whole = get_row(flat_ref, r, rows, width) + bias + total[at * WP : at * WP + width]
        if r in (0, rows - 1):
            rim_ref[r // (rows - 1)] = whole
        else:
            y_ref[r - 1 - skip] = whole.astype(BF16)


def frame0_kernel(tiles, stat_ref, c_hbm, x_hbm, left_ref, right_ref, w_hbm, gain_ref, bias_ref,
                  y_ref, rim_ref, new_ref, v_ref, coef_ref, x_ref, x1_ref, xa_ref,
                  c_ref, x0_ref, sum_ref, pad_ref, flat_ref, frame_sems, sems):
    _, width, rows, chans = x_ref.shape
    copies = {}

    def load_weights(t):
        for a in range(3):
            copies[t, a] = pltpu.make_async_copy(
                w_hbm.at[t, a], v_ref.at[a, :, (2 - t) * chans : (3 - t) * chans], sems.at[t, a])
            copies[t, a].start()

    def wait_weights(t):
        for a in range(3):
            copies[t, a].wait()

    loads = [fetch(x_hbm, 0, x_ref.at[0], frame_sems.at[0]), fetch(c_hbm, 0, c_ref.at[0], frame_sems.at[1])]
    load_weights(0)
    loads.append(fetch(c_hbm, 1, c_ref.at[1], frame_sems.at[2]))
    load_weights(1)
    load_weights(2)
    loads.append(fetch(x_hbm, 1, x_ref.at[1], frame_sems.at[3]))
    firsts = range(0, rows, BLOCK)

    def cached_taps(k, out_ref):
        wait_all(loads[k + 1])
        put_lines(flat_ref, c_ref[k].astype(F32).reshape(width * rows, chans))
        build_taps(flat_ref, left_ref[k], right_ref[k], pad_ref, out_ref, rows, width)

    clear_tail(pad_ref, width)
    cached_taps(0, x0_ref)
    wait_all(loads[0])
    wait_weights(0)
    for first in firsts:
        sum_ref[first * WP : (first + BLOCK) * WP] = product(x0_ref, first, v_ref, 2)
    part = rows * width * (chans // GROUPS)
    count = part * tiles
    stat = stat_ref[...].reshape(tiles, 128)
    moved = pltpu.roll(stat, GROUPS, 1)
    mean = jnp.sum(stat, axis=0, keepdims=True) * (1.0 / count)
    mean_moved = jnp.sum(moved, axis=0, keepdims=True) * (1.0 / count)
    off = moved * (1.0 / part) - mean_moved
    var = jnp.sum(stat + part * off * off, axis=0, keepdims=True) * (1.0 / count)
    lane = lax.broadcasted_iota(jnp.int32, (1, 128), 1)
    is_mean = ((lane >> 5) & 1) == 0
    both = jnp.where(is_mean, mean, lax.rsqrt(jnp.maximum(var, 0.0) + EPS))
    both = jnp.broadcast_to(both, (8, 128))
    gain = gain_ref[...]
    for f in range(2):
        means = exact_dot(both, from_group(chans, 2 * f))[0:1]
        rstds = exact_dot(both, from_group(chans, 2 * f + 1))[0:1]
        scale = rstds * gain
        coef_ref[2 * f : 2 * f + 1, :] = scale
        coef_ref[2 * f + 1 : 2 * f + 2, :] = -means * scale
    frame_taps(0, x_ref, left_ref, right_ref, coef_ref[0:1], coef_ref[1:2], pad_ref, flat_ref, new_ref, xa_ref)
    cached_taps(1, x1_ref)
    wait_weights(1)
    for first in firsts:
        sum_ref[first * WP : (first + BLOCK) * WP] += product(x1_ref, first, v_ref, 1)
    put_lines(flat_ref, x_ref[0].astype(F32).reshape(width * rows, chans))
    wait_weights(2)
    for first in firsts:
        total = sum_ref[first * WP : (first + BLOCK) * WP] + product(xa_ref, first, v_ref, 0)
        finish_rows(total, first, flat_ref, bias_ref[...], width, rows, y_ref, rim_ref)
    wait_all(loads[3])


def edge_part(side, src_ref, v_ref, coef_ref, rim0_ref, rim1_ref, pad_ref, halo_ref):
    _, width, chans = rim0_ref.shape
    row, col = tile_place()
    last = lax.div(lax.axis_size("tile"), TCOL) - 1
    inside = (row > 0) if side == 0 else (row < last)
    clear_tail(pad_ref, width)
    for k in range(4):
        cells = src_ref[k].astype(F32)
        if k >= 2:
            f = k - 2
            cells = activated(cells, coef_ref[2 * f : 2 * f + 1], coef_ref[2 * f + 1 : 2 * f + 2])
        at = lax.broadcasted_iota(jnp.int32, cells.shape, 0)
        keep = (at < width) | ((at == width) & (col > 0)) | ((at == width + 1) & (col < TCOL - 1))
        cells = jnp.where(keep & inside, cells, 0.0)
        pad_ref[k, 8 : 8 + width, :] = cells[0:width]
        pad_ref[k, 7:8, :] = cells[width : width + 1]
        pad_ref[k, 8 + width : 9 + width, :] = cells[width + 1 : width + 2]
        for b in range(3):
            halo_ref[k, :, b * chans : (b + 1) * chans] = pad_ref[k, 7 + b : 7 + b + WP, :].astype(BF16)
    parts = [jnp.dot(halo_ref[k], v_ref[2 * side, :, lo * chans : hi * chans], preferred_element_type=F32)
             for k, (lo, hi) in enumerate(((2, 3), (1, 3), (0, 2), (0, 1)))]
    total0 = parts[0] + parts[1][:, :chans] + parts[2][:, :chans]
    total1 = parts[1][:, chans:] + parts[2][:, chans:] + parts[3]
    return ((rim0_ref[side] + total0[:width]).astype(BF16), (rim1_ref[side] + total1[:width]).astype(BF16))


def half_kernel(side, x_ref, left_ref, right_ref, beyond_ref, v_ref, x1_ref, xa0_ref, coef_ref, bias_ref, rim0_ref, *refs):
    if side == 0:
        y_ref, new_ref, xa_ref, pad_ref, flat_ref, rim1_ref, halo_ref = refs
        frame_taps(1, x_ref, left_ref, right_ref, coef_ref[2:3], coef_ref[3:4], pad_ref, flat_ref, new_ref, xa_ref)
    else:
        xa_ref, y_ref, pad_ref, flat_ref, rim1_ref, halo_ref = refs
    _, width, rows, chans = x_ref.shape
    put_lines(flat_ref, x_ref[1].astype(F32).reshape(width * rows, chans))
    first = side * BLOCK
    total = (product(x1_ref, first, v_ref, 2) + product(xa0_ref, first, v_ref, 1)
             + product(xa_ref, first, v_ref, 0))
    finish_rows(total, first, flat_ref, bias_ref[...], width, rows, y_ref.at[pl.ds(0, BLOCK - 1)], rim1_ref, side * (BLOCK - 1))
    y_ref[BLOCK - 1], y_ref[BLOCK] = edge_part(
        side, beyond_ref, v_ref, coef_ref, rim0_ref, rim1_ref, pad_ref, halo_ref)


def spread_kernel(y0_ref, half_ref, new0_ref, new1_ref, flat_ref, new_ref):
    new_ref[0] = new0_ref[...]
    new_ref[1] = new1_ref[...]
    inner, width, _ = y0_ref.shape
    rows = inner + 2
    for r in range(inner):
        put_row(flat_ref.at[0], r + 1, rows, width, y0_ref[r].astype(F32))
    for f in range(2):
        put_row(flat_ref.at[f], 0, rows, width, half_ref[BLOCK - 1 + f].astype(F32))
    for at in range(BLOCK - 1):
        put_row(flat_ref.at[1], at + 1, rows, width, half_ref[at].astype(F32))


def join_kernel(flat_ref, half_ref, out_ref, scr_ref):
    _, width, rows, chans = out_ref.shape
    line = lax.broadcasted_iota(jnp.int32, (width * rows, LANES), 0) & (rows - 1)
    for f in range(2):
        put_row(scr_ref.at[f], rows - 1, rows, width, half_ref[BLOCK - 1 + f].astype(F32))
    for at in range(BLOCK - 1):
        put_row(scr_ref.at[1], rows - BLOCK + at, rows, width, half_ref[at].astype(F32))
    for f, late in ((0, line == rows - 1), (1, line >= rows - BLOCK)):
        for j in range(flat_ref.shape[1]):
            whole = jnp.where(late, scr_ref[f, j], flat_ref[f, j])
            out_ref[f, :, :, j * LANES : (j + 1) * LANES] = whole.astype(BF16).reshape(width, rows, LANES)


def in_hbm(x):
    return pltpu.with_memory_space_constraint(x, pltpu.HBM)


def on_device(frames_in, cache, kernel, gain, conv_bias):
    x = in_hbm(jnp.transpose(frames_in[0][:, 0], (0, 2, 1, 3)))
    c = in_hbm(jnp.transpose(cache[0][:, 0], (0, 2, 1, 3)))
    frames, width, rows, chans = x.shape
    tiles = lax.axis_size("tile")
    sections = lax.axis_size("section")
    weights = in_hbm(kernel.reshape(3, 3, 3 * chans, chans))
    inner = rows - 2
    sds = jax.ShapeDtypeStruct
    HBM = pl.BlockSpec(memory_space=pltpu.HBM)
    DMA = pltpu.SemaphoreType.DMA

    taps = pltpu.VMEM((rows + 2, WP, 3 * chans), BF16)
    acc = (rows * WP, chans)
    cols = sds((4, rows, chans), F32)
    frame = pltpu.VMEM((width, rows, chans), BF16)
    both = pltpu.VMEM((frames, width, rows, chans), BF16)
    pad = pltpu.VMEM((rows, 80, chans), F32)
    flat = pltpu.VMEM((chans // LANES, width * rows, LANES), F32)
    rim = pltpu.VMEM((2, width, chans), F32)
    edge_rows = sds((4, WP, chans), BF16)

    def call(body, name, us, in_specs, out_specs, out_shape, scratch, aliases={}):
        return pl.pallas_call(body, input_output_aliases=aliases, out_shape=out_shape, in_specs=in_specs, out_specs=out_specs,
                              scratch_shapes=scratch, compiler_params=params(), name=name, cost_estimate=cost(us))

    stat, first_col, last_col = call(
        first_kernel, "local_stats", 1, [HBM] * 2, [VMEM] * 3,
        (sds((tiles, 1, 128), F32), sds((4, rows, chans), BF16), sds((4, rows, chans), BF16)),
        [both, pltpu.VMEM((2, 2, rows, chans), BF16), DMA((2, PARTS)), DMA((2, 2))],
    )(x, c)
    stats = lax.all_to_all(stat, "tile", 0, 0, tiled=True)
    next_col = [(i, i - i % TCOL + (i + 1) % TCOL) for i in range(tiles)]
    next_row = [(i, (i + TCOL) % tiles) for i in range(tiles)]
    back = lambda pairs: [(j, i) for i, j in pairs]
    from_left = lax.ppermute(last_col, "tile", next_col)
    from_right = lax.ppermute(first_col, "tile", back(next_col))
    bottom, top, left, right = call(
        rows_kernel, "pack_rows", 2, [HBM, HBM, VMEM, VMEM], [VMEM] * 4, (edge_rows, edge_rows, cols, cols),
        [pltpu.VMEM((4, width, rows, chans), BF16), flat, DMA((4, PARTS))],
    )(c, x, from_left, from_right)
    above = lax.ppermute(bottom, "tile", next_row)
    below = lax.ppermute(top, "tile", back(next_row))
    onward = [(i, (i + 1) % sections) for i in range(sections)]
    y0, rim0, new0, v, coef, xv, x1, xa0 = call(
        functools.partial(frame0_kernel, tiles), "frame0", 10, [VMEM, HBM, HBM, VMEM, VMEM, HBM, VMEM, VMEM], [VMEM] * 8,
        (sds((inner, width, chans), BF16), rim, frame, pltpu.VMEM((3, 3 * chans, 3 * chans), BF16),
         pltpu.VMEM((8, chans), F32), both, taps, taps),
        [both, taps, pltpu.VMEM(acc, F32), pad, flat, DMA((4, PARTS)), DMA((3, 3))],
    )(stats, c, x, left, right, weights, gain, conv_bias)
    y0 = lax.ppermute(y0, "section", onward)
    half = sds((BLOCK + 1, width, chans), BF16)
    halo = pltpu.VMEM((4, WP, 3 * chans), BF16)
    half_a, new1, xa1 = call(
        functools.partial(half_kernel, 0), "frame1_first", 4, [VMEM] * 10, [VMEM] * 3, (half, frame, taps),
        [pad, flat, rim, halo],
    )(xv, left, right, above, v, x1, xa0, coef, conv_bias, rim0)
    half_a = lax.ppermute(half_a, "section", onward)
    half_b = call(
        functools.partial(half_kernel, 1), "frame1_second", 4, [VMEM] * 11, VMEM, half, [pad, flat, rim, halo],
    )(xv, left, right, below, v, x1, xa0, coef, conv_bias, rim0, xa1)
    half_b = lax.ppermute(half_b, "section", onward)
    spread, new = call(
        spread_kernel, "spread_rows", 10, [VMEM] * 4, [VMEM] * 2,
        (pltpu.VMEM((frames, chans // LANES, width * rows, LANES), F32), sds((frames, width, rows, chans), BF16)), [],
    )(y0, half_a, new0, new1)
    handed = call(
        join_kernel, "join_rows", 1, [VMEM] * 2, VMEM, sds((frames, width, rows, chans), BF16),
        [pltpu.VMEM((frames, chans // LANES, width * rows, LANES), F32)],
    )(spread, half_b)
    handed = jnp.transpose(handed, (0, 2, 1, 3))
    new = jnp.transpose(new, (0, 2, 1, 3))
    return (handed[None, :, None], new[None, :, None])


def solution(mesh):
    tiled = P("section", None, "tile", None, None, None)
    in_specs = (tiled, tiled, P("section", None, None, None, None, None), P("section", None), P("section", None))
    return jax.shard_map(
        on_device, mesh=mesh, in_specs=in_specs, out_specs=(tiled, tiled), check_vma=False
    )
```

time: 254 us -> 55.4 us (0.22)
  blocking collectives: 131 us -> 0 us
  local copies, waits for them, and re-layouts: 46.7 us -> 0.01 us
  Pallas kernels: 0 us -> 24.9 us
  other arithmetic: 24.7 us -> 0 us
  matrix products: 20.8 us -> 0 us
  starting transfers between devices: 10.1 us -> 21.2 us
  waiting for transfers between devices: 19 us -> 8.37 us
    psum x2 -> x0, blocking collectives: 131 us -> none  [the longest x1 65.6 us: on_device(): lax.psum(jnp.sum(deviation * deviation, axis=(1, 2, 4)), 'tile') / count]
    pallas_call x0 -> x7, Pallas kernels: none -> 24.9 us  [the longest x1 10 us: on_device(): call(functools.partial(frame0_kernel, tiles), 'frame0', 10, [VMEM, HBM, H...]
    reshape x9 -> x0, local copies, waits for them, and re-layouts: 22 us -> none  [the longest x8 20.6 us: convolve(): taps = taps.reshape(-1, 3 * chans)]
    dot_general x9 -> x0, matrix products: 20.8 us -> none  [convolve(): total = total + jnp.dot(taps, matrix, preferred_element_type=jnp.float32)]
    concatenate x10 -> x0, other arithmetic: 20.4 us -> none  [the longest x7 13.6 us: convolve(): jnp.concatenate([block[:, :, step_w:step_w + width] for step_w in range(3...]
    slice x3 -> x0, local copies, waits for them, and re-layouts: 13.4 us -> none  [the longest x2 7.73 us: convolve(): block[:, :, step_w:step_w + width]]
    ppermute x5 -> x7, waiting for transfers between devices: 19 us -> 8.37 us  [the longest x1 4.2 us: on_device(): half_a = lax.ppermute(half_a, 'section', onward)]
    all_to_all x0 -> x1, starting transfers between devices: none -> 7.01 us  [on_device(): stats = lax.all_to_all(stat, 'tile', 0, 0, tiled=True)]
  transfers between devices with their start and end apart: 5 -> 8, of which waited for: 1 -> 2; matrix products, arithmetic and copies ran while one was open for 14% -> 0% of each run, Pallas kernels for 0% -> 38%
where the time goes in v2:
time: 55.4 us; the launch traced here: 55.2 us
  Pallas kernels  24.9 us (45%)
  starting transfers between devices  21.2 us (38%)
  waiting for transfers between devices  8.37 us (15%)
  between operations  0.72 us (1%)
    pallas_call x1, Pallas kernels, on_device(): call(functools.partial(frame0_kernel, tiles), 'frame0', 10, [VMEM, HBM, H...  10 us
    all_to_all x1, starting transfers between devices, on_device(): stats = lax.all_to_all(stat, 'tile', 0, 0, tiled=True)  7.01 us
    pallas_call x1, Pallas kernels, on_device(): call(functools.partial(half_kernel, 0), 'frame1_first', 4, [VMEM] * 10, [...  4.3 us
    ppermute x1, waiting for transfers between devices, on_device(): half_a = lax.ppermute(half_a, 'section', onward)  4.2 us
    ppermute x1, waiting for transfers between devices, on_device(): half_b = lax.ppermute(half_b, 'section', onward)  4.15 us
    pallas_call x1, Pallas kernels, on_device(): call(functools.partial(half_kernel, 1), 'frame1_second', 4, [VMEM] * 11,...  4.02 us
    ppermute x1, starting transfers between devices, on_device(): above = lax.ppermute(bottom, 'tile', next_row)  2.97 us
    ppermute x1, starting transfers between devices, on_device(): from_left = lax.ppermute(last_col, 'tile', next_col)  2.68 us
  transfers between devices with their start and end apart: 8, of which 2 were waited for; matrix products, arithmetic and copies ran while one was open for 0% of the time, Pallas kernels for 38%

profile of v2, /device:TPU:1, one launch (start us, length us, event | category | flops | bytes accessed | tf_op | source)
XLA Modules:
  0.0 55.2 jit_solution(12642508764905119928)
XLA Ops:
  0.6 2.6 %local_stats.1 = (f32[32,1,128]{2,1,0:T(1,128)}, bf16[4,8,384]{2,1,0:T(8,128)(2,1)S(1)}, bf16[4,8,384]{2,1,0:T(8,128)(2,1)S(1)}) custom-call(bf16[2,60,8,384]{3,2,1,0:T(8,128)(2,1)} %bitcast.18, bf16[2,60,8,384]{3,2,1,0:T(8,128)(2,1)} %bitcast.21), custom_call_target="tpu_custom_call" | custom-call | flops 1000000000 | bytes 3000000 | tf_op jit(solution)/shard_map/local_stats/pallas_call | solution.py:394
  3.2 2.7 %collective-permute-start = (bf16[4,8,384]{2,1,0:T(8,128)(2,1)S(1)}, bf16[4,8,384]{2,1,0:T(8,128)(2,1)S(1)}, u32[]{:S(2)}, u32[]{:S(2)}) collective-permute-start(bf16[4,8,384]{2,1,0:T(8,128)(2,1)S(1)} %get-tuple-element.23), channel_id=1, source_target_pairs={{0,1},{1,2},{2,3},{3,0},{4,5},{5,6},{6,7},{7,4},{8,9},{9,10},{10,1... | collective-permute-start | bytes 73736 | tf_op jit(solution)/shard_map/ppermute | solution.py:403
  5.9 0.7 %collective-permute-start.1 = (bf16[4,8,384]{2,1,0:T(8,128)(2,1)S(1)}, bf16[4,8,384]{2,1,0:T(8,128)(2,1)S(1)}, u32[]{:S(2)}, u32[]{:S(2)}) collective-permute-start(bf16[4,8,384]{2,1,0:T(8,128)(2,1)S(1)} %get-tuple-element.24), channel_id=1, source_target_pairs={{1,0},{2,1},{3,2},{0,3},{5,4},{6,5},{7,6},{4,7},{9,8},{10,9},{11,1... | collective-permute-start | bytes 73736 | tf_op jit(solution)/shard_map/ppermute | solution.py:404
  6.6 7.0 %all-to-all-start = ((f32[32,1,128]{2,1,0:T(1,128)}), f32[32,1,128]{2,1,0:T(1,128)S(1)}, u32[]{:S(2)}, u32[]{:S(2)}) async-start(f32[32,1,128]{2,1,0:T(1,128)} %get-tuple-element.22), calls=%async_computation | async-start | bytes 32768 | tf_op jit(solution)/shard_map/all_to_all | solution.py:399
  13.6 0.0 copy-start
  13.6 0.0 copy-start.1
  13.7 0.0 collective-permute-done.from_left_ref
  13.7 0.0 collective-permute-done.1.from_right_ref
  13.7 1.6 %pack_rows.1 = (bf16[4,64,384]{2,1,0:T(8,128)(2,1)S(1)}, bf16[4,64,384]{2,1,0:T(8,128)(2,1)S(1)}, f32[4,8,384]{2,1,0:T(8,128)S(1)}, f32[4,8,384]{2,1,0:T(8,128)S(1)}) custom-call(bf16[2,60,8,384]{3,2,1,0:T(8,128)(2,1)} %bitcast.22, bf16[2,60,8,384]{3,2,1,0:T(8,128)(2,1)} %bitcast.19, bf16[4,8,384]{2,1,0:T(8,128)(2,1)S(1)} %collective-permute-done.from_left_ref, ...), custom_call_target="tpu_custom_call" | custom-call | flops 2000000000 | bytes 6000000 | tf_op jit(solution)/shard_map/pack_rows/pallas_call | solution.py:405
  15.3 3.0 %collective-permute-start.3 = (bf16[4,64,384]{2,1,0:T(8,128)(2,1)S(1)}, bf16[4,64,384]{2,1,0:T(8,128)(2,1)S(1)}, u32[]{:S(2)}, u32[]{:S(2)}) collective-permute-start(bf16[4,64,384]{2,1,0:T(8,128)(2,1)S(1)} %get-tuple-element.29), channel_id=1, source_target_pairs={{0,4},{1,5},{2,6},{3,7},{4,8},{5,9},{6,10},{7,11},{8,12},{9,13},{1... | collective-permute-start | bytes 589832 | tf_op jit(solution)/shard_map/ppermute | solution.py:409
  18.3 2.5 %collective-permute-start.5 = (bf16[4,64,384]{2,1,0:T(8,128)(2,1)S(1)}, bf16[4,64,384]{2,1,0:T(8,128)(2,1)S(1)}, u32[]{:S(2)}, u32[]{:S(2)}) collective-permute-start(bf16[4,64,384]{2,1,0:T(8,128)(2,1)S(1)} %get-tuple-element.39), channel_id=1, source_target_pairs={{4,0},{5,1},{6,2},{7,3},{8,4},{9,5},{10,6},{11,7},{12,8},{13,9},{1... | collective-permute-start | bytes 589832 | tf_op jit(solution)/shard_map/ppermute | solution.py:410
  20.7 0.0 all-to-all-done.stat_ref
  20.7 0.0 copy-done
  20.8 0.0 copy-done.1
  20.8 10.0 %frame0.1 = (bf16[6,60,384]{2,1,0:T(8,128)(2,1)S(1)}, f32[2,60,384]{2,1,0:T(8,128)S(1)}, bf16[60,8,384]{2,1,0:T(8,128)(2,1)S(1)}, bf16[3,1152,1152]{2,1,0:T(8,12...) custom-call(f32[32,1,128]{2,1,0:T(1,128)S(1)} %all-to-all-done.stat_, ...), custom_call_target="tpu_custom_call" | custom-call | flops 10000000000 | bytes 30000000 | tf_op jit(solution)/shard_map/frame0/pallas_call | solution.py:412
  30.8 1.9 %collective-permute-start.2 = (bf16[6,60,384]{2,1,0:T(8,128)(2,1)S(1)}, bf16[6,60,384]{2,1,0:T(8,128)(2,1)S(1)}, u32[]{:S(2)}, u32[]{:S(2)}) collective-permute-start(bf16[6,60,384]{2,1,0:T(8,128)(2,1)S(1)} %get-tuple-element.27), channel_id=1, source_target_pairs={{0,32},{32,64},{64,96},{96,128},{128,160},{160,192},{192,224},{224... | collective-permute-start | bytes 829448 | tf_op jit(solution)/shard_map/ppermute | solution.py:418
  32.7 0.0 collective-permute-done.3.beyond_ref
  32.7 4.3 %frame1_first.1 = (bf16[5,60,384]{2,1,0:T(8,128)(2,1)S(1)}, bf16[60,8,384]{2,1,0:T(8,128)(2,1)S(1)}, bf16[10,64,1152]{2,1,0:T(8,128)(2,1)S(1)}) custom-call(bf16[2,60,8,384]{3,2,1,0:T(8,128)(2,1)S(1)} %get-tuple-element.28.x_ref, f32[4,8,384]{2,1,0:T(8,128)S(1)} %get-tuple-element.25.left_ref, f32[4,8,384]{2,1,0:T(8,128)S(1)} %get-tuple-element.26.right_ref, ...), custom_call_target="tpu_custom_call" | custom-call | flops 4000000000 | bytes 12000000 | tf_op jit(solution)/shard_map/frame1_first/pallas_call | solution.py:421
  37.0 1.7 %collective-permute-start.4 = (bf16[5,60,384]{2,1,0:T(8,128)(2,1)S(1)}, bf16[5,60,384]{2,1,0:T(8,128)(2,1)S(1)}, u32[]{:S(2)}, u32[]{:S(2)}) collective-permute-start(bf16[5,60,384]{2,1,0:T(8,128)(2,1)S(1)} %get-tuple-element.35), channel_id=1, source_target_pairs={{0,32},{32,64},{64,96},{96,128},{128,160},{160,192},{192,224},{224... | collective-permute-start | bytes 691208 | tf_op jit(solution)/shard_map/ppermute | solution.py:425
  38.7 0.0 collective-permute-done.5.beyond_ref
  38.7 4.0 %frame1_second.1 = bf16[5,60,384]{2,1,0:T(8,128)(2,1)S(1)} custom-call(bf16[2,60,8,384]{3,2,1,0:T(8,128)(2,1)S(1)} %get-tuple-element.28.x_ref, f32[4,8,384]{2,1,0:T(8,128)S(1)} %get-tuple-element.25.left_ref, f32[4,8,384]{2,1,0:T(8,128)S(1)} %get-tuple-element.26.right_ref, bf16[4,64,384]{2,1,0:T(8,128)(2,1)S(1)} %collective-permute-done.5.beyond_ref, ...), custom_call_target="tpu_custom_call" | custom-call | flops 4000000000 | bytes 12000000 | tf_op jit(solution)/shard_map/frame1_second/pallas_call | solution.py:426
  42.8 1.7 %collective-permute-start.6 = (bf16[5,60,384]{2,1,0:T(8,128)(2,1)S(1)}, bf16[5,60,384]{2,1,0:T(8,128)(2,1)S(1)}, u32[]{:S(2)}, u32[]{:S(2)}) collective-permute-start(bf16[5,60,384]{2,1,0:T(8,128)(2,1)S(1)} %frame1_second.1), channel_id=1, source_target_pairs={{0,32},{32,64},{64,96},{96,128},{128,160},{160,192},{192,224},{224... | collective-permute-start | bytes 691208 | tf_op jit(solution)/shard_map/ppermute | solution.py:429
  44.5 0.0 collective-permute-done.2.y0_ref
  44.5 4.2 %collective-permute-done.4.half_ref = bf16[5,60,384]{2,1,0:T(8,128)(2,1)S(1)} collective-permute-done((bf16[5,60,384]{2,1,0:T(8,128)(2,1)S(1)}, bf16[5,60,384]{2,1,0:T(8,128)(2,1)S(1)}, u32[]{:S(2)}, u32[]{:S(2)}) %collective-permute-start.4) | collective-permute-done | bytes 230432 | tf_op jit(solution)/shard_map/ppermute | solution.py:425
  48.7 1.1 %spread_rows.1 = (f32[2,3,480,128]{3,2,1,0:T(8,128)S(1)}, bf16[2,60,8,384]{3,2,1,0:T(8,128)(2,1)}) custom-call(bf16[6,60,384]{2,1,0:T(8,128)(2,1)S(1)} %collective-permute-done.2.y0_ref, bf16[5,60,384]{2,1,0:T(8,128)(2,1)S(1)} %collective-permute-done.4.half_ref, bf16[60,8,384]{2,1,0:T(8,128)(2,1)S(1)} %get-tuple-element.36.new0_ref, ...), custom_call_target="tpu_custom_call" | custom-call | flops 10000000000 | bytes 30000000 | tf_op jit(solution)/shard_map/spread_rows/pallas_call | solution.py:430
  49.8 4.2 %collective-permute-done.6.half_ref = bf16[5,60,384]{2,1,0:T(8,128)(2,1)S(1)} collective-permute-done((bf16[5,60,384]{2,1,0:T(8,128)(2,1)S(1)}, bf16[5,60,384]{2,1,0:T(8,128)(2,1)S(1)}, u32[]{:S(2)}, u32[]{:S(2)}) %collective-permute-start.6) | collective-permute-done | bytes 230432 | tf_op jit(solution)/shard_map/ppermute | solution.py:429
  53.9 1.2 %join_rows.1 = bf16[2,60,8,384]{3,2,1,0:T(8,128)(2,1)} custom-call(f32[2,3,480,128]{3,2,1,0:T(8,128)S(1)} %get-tuple-element.38.flat_ref, bf16[5,60,384]{2,1,0:T(8,128)(2,1)S(1)} %collective-permute-done.6.half_ref), custom_call_target="tpu_custom_call" | custom-call | flops 1000000000 | bytes 3000000 | tf_op jit(solution)/shard_map/join_rows/pallas_call | solution.py:434
Async XLA Ops:
  3.2 10.4 %collective-permute-start = (bf16[4,8,384]{2,1,0:T(8,128)(2,1)S(1)}, bf16[4,8,384]{2,1,0:T(8,128)(2,1)S(1)}, u32[]{:S(2)}, u32[]{:S(2)}) collective-permute-start(bf16[4,8,384]{2,1,0:T(8,128)(2,1)S(1)} %get-tuple-element.23), channel_id=1, source_target_pairs={{0,1},{1,2},{2,3},{3,0},{4,5},{5,6},{6,7},{7,4},{8,9},{9,10},{10,1... | collective-permute-start | bytes 73736 | tf_op jit(solution)/shard_map/ppermute | solution.py:403
  5.9 7.8 %collective-permute-start.1 = (bf16[4,8,384]{2,1,0:T(8,128)(2,1)S(1)}, bf16[4,8,384]{2,1,0:T(8,128)(2,1)S(1)}, u32[]{:S(2)}, u32[]{:S(2)}) collective-permute-start(bf16[4,8,384]{2,1,0:T(8,128)(2,1)S(1)} %get-tuple-element.24), channel_id=1, source_target_pairs={{1,0},{2,1},{3,2},{0,3},{5,4},{6,5},{7,6},{4,7},{9,8},{10,9},{11,1... | collective-permute-start | bytes 73736 | tf_op jit(solution)/shard_map/ppermute | solution.py:404
  6.6 14.1 %all-to-all-start = ((f32[32,1,128]{2,1,0:T(1,128)}), f32[32,1,128]{2,1,0:T(1,128)S(1)}, u32[]{:S(2)}, u32[]{:S(2)}) async-start(f32[32,1,128]{2,1,0:T(1,128)} %get-tuple-element.22), calls=%async_computation | async-start | bytes 32768 | tf_op jit(solution)/shard_map/all_to_all | solution.py:399
  13.6 7.1 %copy-start = (f32[1,384]{1,0:T(1,128)S(1)}, f32[1,384]{1,0:T(1,128)}, u32[]{:S(2)}) copy-start(f32[1,384]{1,0:T(1,128)} %gain_ref.1) | copy-start | bytes 4612
  13.6 7.1 %copy-start.1 = (f32[1,384]{1,0:T(1,128)S(1)}, f32[1,384]{1,0:T(1,128)}, u32[]{:S(2)}) copy-start(f32[1,384]{1,0:T(1,128)} %bias_ref.5) | copy-start | bytes 4612
  15.3 17.4 %collective-permute-start.3 = (bf16[4,64,384]{2,1,0:T(8,128)(2,1)S(1)}, bf16[4,64,384]{2,1,0:T(8,128)(2,1)S(1)}, u32[]{:S(2)}, u32[]{:S(2)}) collective-permute-start(bf16[4,64,384]{2,1,0:T(8,128)(2,1)S(1)} %get-tuple-element.29), channel_id=1, source_target_pairs={{0,4},{1,5},{2,6},{3,7},{4,8},{5,9},{6,10},{7,11},{8,12},{9,13},{1... | collective-permute-start | bytes 589832 | tf_op jit(solution)/shard_map/ppermute | solution.py:409
  18.3 20.4 %collective-permute-start.5 = (bf16[4,64,384]{2,1,0:T(8,128)(2,1)S(1)}, bf16[4,64,384]{2,1,0:T(8,128)(2,1)S(1)}, u32[]{:S(2)}, u32[]{:S(2)}) collective-permute-start(bf16[4,64,384]{2,1,0:T(8,128)(2,1)S(1)} %get-tuple-element.39), channel_id=1, source_target_pairs={{4,0},{5,1},{6,2},{7,3},{8,4},{9,5},{10,6},{11,7},{12,8},{13,9},{1... | collective-permute-start | bytes 589832 | tf_op jit(solution)/shard_map/ppermute | solution.py:410
  30.8 13.7 %collective-permute-start.2 = (bf16[6,60,384]{2,1,0:T(8,128)(2,1)S(1)}, bf16[6,60,384]{2,1,0:T(8,128)(2,1)S(1)}, u32[]{:S(2)}, u32[]{:S(2)}) collective-permute-start(bf16[6,60,384]{2,1,0:T(8,128)(2,1)S(1)} %get-tuple-element.27), channel_id=1, source_target_pairs={{0,32},{32,64},{64,96},{96,128},{128,160},{160,192},{192,224},{224... | collective-permute-start | bytes 829448 | tf_op jit(solution)/shard_map/ppermute | solution.py:418
  37.0 11.7 %collective-permute-start.4 = (bf16[5,60,384]{2,1,0:T(8,128)(2,1)S(1)}, bf16[5,60,384]{2,1,0:T(8,128)(2,1)S(1)}, u32[]{:S(2)}, u32[]{:S(2)}) collective-permute-start(bf16[5,60,384]{2,1,0:T(8,128)(2,1)S(1)} %get-tuple-element.35), channel_id=1, source_target_pairs={{0,32},{32,64},{64,96},{96,128},{128,160},{160,192},{192,224},{224... | collective-permute-start | bytes 691208 | tf_op jit(solution)/shard_map/ppermute | solution.py:425
  42.8 11.2 %collective-permute-start.6 = (bf16[5,60,384]{2,1,0:T(8,128)(2,1)S(1)}, bf16[5,60,384]{2,1,0:T(8,128)(2,1)S(1)}, u32[]{:S(2)}, u32[]{:S(2)}) collective-permute-start(bf16[5,60,384]{2,1,0:T(8,128)(2,1)S(1)} %frame1_second.1), channel_id=1, source_target_pairs={{0,32},{32,64},{64,96},{96,128},{128,160},{160,192},{192,224},{224... | collective-permute-start | bytes 691208 | tf_op jit(solution)/shard_map/ppermute | solution.py:429

commit v3 on v2

--- a/solution.py
+++ b/solution.py
@@ -42,15 +42,19 @@
     return got[0:8] + got[16:24] + got[32:40]
 
 
-def to_group(chans, block):
+def to_group(chans):
     size = chans // GROUPS
     chan = lax.broadcasted_iota(jnp.int32, (chans, 128), 0)
-    lane = lax.broadcasted_iota(jnp.int32, (chans, 128), 1)
-    first = (lane & (GROUPS - 1)) * size
-    hit = (chan >= first) & (chan < first + size)
-    if block is not None:
-        hit = hit & ((lane >> 5) == block)
-    return jnp.where(hit, 1.0, 0.0).astype(BF16)
+    first = (lax.broadcasted_iota(jnp.int32, (chans, 128), 1) & (GROUPS - 1)) * size
+    return jnp.where((chan >= first) & (chan < first + size), 1.0, 0.0).astype(BF16)
+
+
+def same_group(chans):
+    size = chans // GROUPS
+    row = lax.broadcasted_iota(jnp.int32, (chans, 1), 0)
+    col = lax.broadcasted_iota(jnp.int32, (1, chans), 1)
+    of = lambda c: (c * ((1 << 18) // size + 1)) >> 18
+    return jnp.where(of(row) == of(col), 1.0, 0.0).astype(BF16)
 
 
 def from_group(chans, block):
@@ -90,6 +94,7 @@
         copy.start()
     size = chans // GROUPS
     count = rows * width
+    every, same = to_group(chans), same_group(chans)
     sums, squares = [], []
     for f in range(frames):
         wait_all(loads[f])
@@ -104,13 +109,11 @@
         last_ref[k] = edge_ref[k, 1] if k < 2 else x_ref[k - 2, width - 1]
     zero = jnp.zeros((1, chans), F32)
     both = jnp.concatenate(sums + [zero] * 6, axis=0)
-    grouped = exact_dot(both, to_group(chans, 0))
-    spread = exact_dot(grouped, from_group(chans, 0))
+    spread = exact_dot(both, same)
     off = both * (1.0 / count) - spread * (1.0 / (count * size))
     square = jnp.concatenate(squares + [zero] * 6, axis=0) + count * off * off
     row = lax.broadcasted_iota(jnp.int32, (8, 128), 0)
     lane = lax.broadcasted_iota(jnp.int32, (8, 128), 1)
-    every = to_group(chans, None)
     mix_sum = exact_dot(both, every)
     mix_square = exact_dot(square, every)
     kind = lane >> 5
@@ -216,23 +219,28 @@
     build_taps(flat_ref, left, right, pad_ref, out_ref, rows, width)
 
 
-def finish_rows(total, first, flat_ref, bias, width, rows, y_ref, rim_ref, skip=0):
+def put_cells(line_ref, at, value):
+    line_ref[at * value.shape[0] : (at + 1) * value.shape[0], :] = value
+
+
+def finish_rows(total, first, flat_ref, bias, width, rows, line_ref, rim_ref, skip=0):
     for at in range(BLOCK):
         r = first + at
         whole = get_row(flat_ref, r, rows, width) + bias + total[at * WP : at * WP + width]
         if r in (0, rows - 1):
             rim_ref[r // (rows - 1)] = whole
         else:
-            y_ref[r - 1 - skip] = whole.astype(BF16)
+            put_cells(line_ref, r - 1 - skip, whole)
 
 
 def frame0_kernel(tiles, stat_ref, c_hbm, x_hbm, left_ref, right_ref, w_hbm, gain_ref, bias_ref,
                   y_ref, rim_ref, new_ref, v_ref, coef_ref, x_ref, x1_ref, xa_ref,
-                  c_ref, x0_ref, sum_ref, pad_ref, flat_ref, frame_sems, sems):
+                  c_ref, x0_ref, sum_ref, pad_ref, flat_ref, line_ref, frame_sems, sems):
     _, width, rows, chans = x_ref.shape
+    loads = [fetch(c_hbm, 0, c_ref.at[0], frame_sems.at[0]), fetch(c_hbm, 1, c_ref.at[1], frame_sems.at[1]),
+             fetch(x_hbm, 0, x_ref.at[0], frame_sems.at[2])]
     copies = {}
-
-    def load_weights(t):
+    for t in range(3):
         for a in range(3):
             copies[t, a] = pltpu.make_async_copy(
                 w_hbm.at[t, a], v_ref.at[a, :, (2 - t) * chans : (3 - t) * chans], sems.at[t, a])
@@ -242,25 +250,7 @@
         for a in range(3):
             copies[t, a].wait()
 
-    loads = [fetch(x_hbm, 0, x_ref.at[0], frame_sems.at[0]), fetch(c_hbm, 0, c_ref.at[0], frame_sems.at[1])]
-    load_weights(0)
-    loads.append(fetch(c_hbm, 1, c_ref.at[1], frame_sems.at[2]))
-    load_weights(1)
-    load_weights(2)
     loads.append(fetch(x_hbm, 1, x_ref.at[1], frame_sems.at[3]))
-    firsts = range(0, rows, BLOCK)
-
-    def cached_taps(k, out_ref):
-        wait_all(loads[k + 1])
-        put_lines(flat_ref, c_ref[k].astype(F32).reshape(width * rows, chans))
-        build_taps(flat_ref, left_ref[k], right_ref[k], pad_ref, out_ref, rows, width)
-
-    clear_tail(pad_ref, width)
-    cached_taps(0, x0_ref)
-    wait_all(loads[0])
-    wait_weights(0)
-    for first in firsts:
-        sum_ref[first * WP : (first + BLOCK) * WP] = product(x0_ref, first, v_ref, 2)
     part = rows * width * (chans // GROUPS)
     count = part * tiles
     stat = stat_ref[...].reshape(tiles, 128)
@@ -280,16 +270,26 @@
         scale = rstds * gain
         coef_ref[2 * f : 2 * f + 1, :] = scale
         coef_ref[2 * f + 1 : 2 * f + 2, :] = -means * scale
+    clear_tail(pad_ref, width)
+    for k, out_ref in ((0, x0_ref), (1, x1_ref)):
+        wait_all(loads[k])
+        put_lines(flat_ref, c_ref[k].astype(F32).reshape(width * rows, chans))
+        build_taps(flat_ref, left_ref[k], right_ref[k], pad_ref, out_ref, rows, width)
+    wait_all(loads[2])
     frame_taps(0, x_ref, left_ref, right_ref, coef_ref[0:1], coef_ref[1:2], pad_ref, flat_ref, new_ref, xa_ref)
-    cached_taps(1, x1_ref)
+    put_lines(flat_ref, x_ref[0].astype(F32).reshape(width * rows, chans))
+    firsts = range(0, rows, BLOCK)
+    wait_weights(0)
+    for first in firsts:
+        sum_ref[first * WP : (first + BLOCK) * WP] = product(x0_ref, first, v_ref, 2)
     wait_weights(1)
     for first in firsts:
         sum_ref[first * WP : (first + BLOCK) * WP] += product(x1_ref, first, v_ref, 1)
-    put_lines(flat_ref, x_ref[0].astype(F32).reshape(width * rows, chans))
     wait_weights(2)
     for first in firsts:
         total = sum_ref[first * WP : (first + BLOCK) * WP] + product(xa_ref, first, v_ref, 0)
-        finish_rows(total, first, flat_ref, bias_ref[...], width, rows, y_ref, rim_ref)
+        finish_rows(total, first, flat_ref, bias_ref[...], width, rows, line_ref, rim_ref)
+    y_ref[...] = line_ref[...].astype(BF16)
     wait_all(loads[3])
 
 
@@ -316,49 +316,55 @@
              for k, (lo, hi) in enumerate(((2, 3), (1, 3), (0, 2), (0, 1)))]
     total0 = parts[0] + parts[1][:, :chans] + parts[2][:, :chans]
     total1 = parts[1][:, chans:] + parts[2][:, chans:] + parts[3]
-    return ((rim0_ref[side] + total0[:width]).astype(BF16), (rim1_ref[side] + total1[:width]).astype(BF16))
+    return rim0_ref[side] + total0[:width], rim1_ref[side] + total1[:width]
 
 
 def half_kernel(side, x_ref, left_ref, right_ref, beyond_ref, v_ref, x1_ref, xa0_ref, coef_ref, bias_ref, rim0_ref, *refs):
     if side == 0:
-        y_ref, new_ref, xa_ref, pad_ref, flat_ref, rim1_ref, halo_ref = refs
+        y_ref, new_ref, xa_ref, pad_ref, flat_ref, rim1_ref, halo_ref, line_ref = refs
         frame_taps(1, x_ref, left_ref, right_ref, coef_ref[2:3], coef_ref[3:4], pad_ref, flat_ref, new_ref, xa_ref)
     else:
-        xa_ref, y_ref, pad_ref, flat_ref, rim1_ref, halo_ref = refs
+        xa_ref, y_ref, pad_ref, flat_ref, rim1_ref, halo_ref, line_ref = refs
     _, width, rows, chans = x_ref.shape
     put_lines(flat_ref, x_ref[1].astype(F32).reshape(width * rows, chans))
     first = side * BLOCK
     total = (product(x1_ref, first, v_ref, 2) + product(xa0_ref, first, v_ref, 1)
              + product(xa_ref, first, v_ref, 0))
-    finish_rows(total, first, flat_ref, bias_ref[...], width, rows, y_ref.at[pl.ds(0, BLOCK - 1)], rim1_ref, side * (BLOCK - 1))
-    y_ref[BLOCK - 1], y_ref[BLOCK] = edge_part(
-        side, beyond_ref, v_ref, coef_ref, rim0_ref, rim1_ref, pad_ref, halo_ref)
+    finish_rows(total, first, flat_ref, bias_ref[...], width, rows, line_ref, rim1_ref, side * (BLOCK - 1))
+    for f, row in enumerate(edge_part(side, beyond_ref, v_ref, coef_ref, rim0_ref, rim1_ref, pad_ref, halo_ref)):
+        put_cells(line_ref, BLOCK - 1 + f, row)
+    y_ref[...] = line_ref[...].astype(BF16)
 
 
 def spread_kernel(y0_ref, half_ref, new0_ref, new1_ref, flat_ref, new_ref):
     new_ref[0] = new0_ref[...]
     new_ref[1] = new1_ref[...]
-    inner, width, _ = y0_ref.shape
-    rows = inner + 2
-    for r in range(inner):
-        put_row(flat_ref.at[0], r + 1, rows, width, y0_ref[r].astype(F32))
+    _, width, rows, _ = new_ref.shape
+    y0, half = y0_ref[...].astype(F32), half_ref[...].astype(F32)
+    for r in range(rows - 2):
+        put_row(flat_ref.at[0], r + 1, rows, width, y0[r * width : (r + 1) * width])
     for f in range(2):
-        put_row(flat_ref.at[f], 0, rows, width, half_ref[BLOCK - 1 + f].astype(F32))
+        put_row(flat_ref.at[f], 0, rows, width, half[(BLOCK - 1 + f) * width : (BLOCK + f) * width])
     for at in range(BLOCK - 1):
-        put_row(flat_ref.at[1], at + 1, rows, width, half_ref[at].astype(F32))
-
-
-def join_kernel(flat_ref, half_ref, out_ref, scr_ref):
+        put_row(flat_ref.at[1], at + 1, rows, width, half[at * width : (at + 1) * width])
+
+
+def join_kernel(flat_ref, half_ref, out_hbm, scr_ref, out_ref, sems):
     _, width, rows, chans = out_ref.shape
     line = lax.broadcasted_iota(jnp.int32, (width * rows, LANES), 0) & (rows - 1)
-    for f in range(2):
-        put_row(scr_ref.at[f], rows - 1, rows, width, half_ref[BLOCK - 1 + f].astype(F32))
-    for at in range(BLOCK - 1):
-        put_row(scr_ref.at[1], rows - BLOCK + at, rows, width, half_ref[at].astype(F32))
+    half = half_ref[...].astype(F32)
+    copies = []
     for f, late in ((0, line == rows - 1), (1, line >= rows - BLOCK)):
+        put_row(scr_ref.at[f], rows - 1, rows, width, half[(BLOCK - 1 + f) * width : (BLOCK + f) * width])
+        if f == 1:
+            for at in range(BLOCK - 1):
+                put_row(scr_ref.at[1], rows - BLOCK + at, rows, width, half[at * width : (at + 1) * width])
         for j in range(flat_ref.shape[1]):
             whole = jnp.where(late, scr_ref[f, j], flat_ref[f, j])
             out_ref[f, :, :, j * LANES : (j + 1) * LANES] = whole.astype(BF16).reshape(width, rows, LANES)
+        copies.append(pltpu.make_async_copy(out_ref.at[f], out_hbm.at[f], sems.at[f]))
+        copies[-1].start()
+    wait_all(copies)
 
 
 def in_hbm(x):
@@ -411,20 +417,22 @@
     onward = [(i, (i + 1) % sections) for i in range(sections)]
     y0, rim0, new0, v, coef, xv, x1, xa0 = call(
         functools.partial(frame0_kernel, tiles), "frame0", 10, [VMEM, HBM, HBM, VMEM, VMEM, HBM, VMEM, VMEM], [VMEM] * 8,
-        (sds((inner, width, chans), BF16), rim, frame, pltpu.VMEM((3, 3 * chans, 3 * chans), BF16),
+        (sds((inner * width, chans), BF16), rim, frame, pltpu.VMEM((3, 3 * chans, 3 * chans), BF16),
          pltpu.VMEM((8, chans), F32), both, taps, taps),
-        [both, taps, pltpu.VMEM(acc, F32), pad, flat, DMA((4, PARTS)), DMA((3, 3))],
+        [both, taps, pltpu.VMEM(acc, F32), pad, flat, pltpu.VMEM((inner * width, chans), F32),
+         DMA((4, PARTS)), DMA((3, 3))],
     )(stats, c, x, left, right, weights, gain, conv_bias)
     y0 = lax.ppermute(y0, "section", onward)
-    half = sds((BLOCK + 1, width, chans), BF16)
+    half = sds(((BLOCK + 1) * width, chans), BF16)
+    lines = pltpu.VMEM(((BLOCK + 1) * width, chans), F32)
     halo = pltpu.VMEM((4, WP, 3 * chans), BF16)
     half_a, new1, xa1 = call(
         functools.partial(half_kernel, 0), "frame1_first", 4, [VMEM] * 10, [VMEM] * 3, (half, frame, taps),
-        [pad, flat, rim, halo],
+        [pad, flat, rim, halo, lines],
     )(xv, left, right, above, v, x1, xa0, coef, conv_bias, rim0)
     half_a = lax.ppermute(half_a, "section", onward)
     half_b = call(
-        functools.partial(half_kernel, 1), "frame1_second", 4, [VMEM] * 11, VMEM, half, [pad, flat, rim, halo],
+        functools.partial(half_kernel, 1), "frame1_second", 4, [VMEM] * 11, VMEM, half, [pad, flat, rim, halo, lines],
     )(xv, left, right, below, v, x1, xa0, coef, conv_bias, rim0, xa1)
     half_b = lax.ppermute(half_b, "section", onward)
     spread, new = call(
@@ -432,8 +440,8 @@
         (pltpu.VMEM((frames, chans // LANES, width * rows, LANES), F32), sds((frames, width, rows, chans), BF16)), [],
     )(y0, half_a, new0, new1)
     handed = call(
-        join_kernel, "join_rows", 1, [VMEM] * 2, VMEM, sds((frames, width, rows, chans), BF16),
-        [pltpu.VMEM((frames, chans // LANES, width * rows, LANES), F32)],
+        join_kernel, "join_rows", 1, [VMEM] * 2, HBM, sds((frames, width, rows, chans), BF16),
+        [pltpu.VMEM((frames, chans // LANES, width * rows, LANES), F32), both, DMA((2,))],
     )(spread, half_b)
     handed = jnp.transpose(handed, (0, 2, 1, 3))
     new = jnp.transpose(new, (0, 2, 1, 3))

time: 55.4 us -> 54.1 us (0.977)
  Pallas kernels: 24.9 us -> 23.8 us
where the time goes in v3:
time: 54.1 us; the launch traced here: 53.8 us
  Pallas kernels  23.8 us (44%)
  starting transfers between devices  21.2 us (39%)
  waiting for transfers between devices  7.9 us (15%)
  between operations  0.9 us (2%)
    pallas_call x1, Pallas kernels, on_device(): call(functools.partial(frame0_kernel, tiles), 'frame0', 10, [VMEM, HBM, H...  9.6 us
    all_to_all x1, starting transfers between devices, on_device(): stats = lax.all_to_all(stat, 'tile', 0, 0, tiled=True)  7.01 us
    pallas_call x1, Pallas kernels, on_device(): call(functools.partial(half_kernel, 0), 'frame1_first', 4, [VMEM] * 10, [...  4.13 us
    ppermute x1, waiting for transfers between devices, on_device(): half_b = lax.ppermute(half_b, 'section', onward)  3.98 us
    ppermute x1, waiting for transfers between devices, on_device(): half_a = lax.ppermute(half_a, 'section', onward)  3.9 us
    pallas_call x1, Pallas kernels, on_device(): call(functools.partial(half_kernel, 1), 'frame1_second', 4, [VMEM] * 11,...  3.84 us
    ppermute x1, starting transfers between devices, on_device(): above = lax.ppermute(bottom, 'tile', next_row)  2.97 us
    ppermute x1, starting transfers between devices, on_device(): from_left = lax.ppermute(last_col, 'tile', next_col)  2.68 us
  transfers between devices with their start and end apart: 8, of which 2 were waited for; matrix products, arithmetic and copies ran while one was open for 0% of the time, Pallas kernels for 38%

profile of v3, /device:TPU:1, one launch (start us, length us, event | category | flops | bytes accessed | tf_op | source)
XLA Modules:
  0.0 53.8 jit_solution(14489217090116183684)
XLA Ops:
  0.6 2.5 %local_stats.1 = (f32[32,1,128]{2,1,0:T(1,128)}, bf16[4,8,384]{2,1,0:T(8,128)(2,1)S(1)}, bf16[4,8,384]{2,1,0:T(8,128)(2,1)S(1)}) custom-call(bf16[2,60,8,384]{3,2,1,0:T(8,128)(2,1)} %bitcast.18, bf16[2,60,8,384]{3,2,1,0:T(8,128)(2,1)} %bitcast.21), custom_call_target="tpu_custom_call" | custom-call | flops 1000000000 | bytes 3000000 | tf_op jit(solution)/shard_map/local_stats/pallas_call | solution.py:400
  3.1 2.7 %collective-permute-start = (bf16[4,8,384]{2,1,0:T(8,128)(2,1)S(1)}, bf16[4,8,384]{2,1,0:T(8,128)(2,1)S(1)}, u32[]{:S(2)}, u32[]{:S(2)}) collective-permute-start(bf16[4,8,384]{2,1,0:T(8,128)(2,1)S(1)} %get-tuple-element.23), channel_id=1, source_target_pairs={{0,1},{1,2},{2,3},{3,0},{4,5},{5,6},{6,7},{7,4},{8,9},{9,10},{10,1... | collective-permute-start | bytes 73736 | tf_op jit(solution)/shard_map/ppermute | solution.py:409
  5.8 0.7 %collective-permute-start.1 = (bf16[4,8,384]{2,1,0:T(8,128)(2,1)S(1)}, bf16[4,8,384]{2,1,0:T(8,128)(2,1)S(1)}, u32[]{:S(2)}, u32[]{:S(2)}) collective-permute-start(bf16[4,8,384]{2,1,0:T(8,128)(2,1)S(1)} %get-tuple-element.24), channel_id=1, source_target_pairs={{1,0},{2,1},{3,2},{0,3},{5,4},{6,5},{7,6},{4,7},{9,8},{10,9},{11,1... | collective-permute-start | bytes 73736 | tf_op jit(solution)/shard_map/ppermute | solution.py:410
  6.5 7.0 %all-to-all-start = ((f32[32,1,128]{2,1,0:T(1,128)}), f32[32,1,128]{2,1,0:T(1,128)S(1)}, u32[]{:S(2)}, u32[]{:S(2)}) async-start(f32[32,1,128]{2,1,0:T(1,128)} %get-tuple-element.22), calls=%async_computation | async-start | bytes 32768 | tf_op jit(solution)/shard_map/all_to_all | solution.py:405
  13.5 0.0 copy-start
  13.5 0.0 copy-start.1
  13.5 0.0 collective-permute-done.from_left_ref
  13.6 0.0 collective-permute-done.1.from_right_ref
  13.6 1.6 %pack_rows.1 = (bf16[4,64,384]{2,1,0:T(8,128)(2,1)S(1)}, bf16[4,64,384]{2,1,0:T(8,128)(2,1)S(1)}, f32[4,8,384]{2,1,0:T(8,128)S(1)}, f32[4,8,384]{2,1,0:T(8,128)S(1)}) custom-call(bf16[2,60,8,384]{3,2,1,0:T(8,128)(2,1)} %bitcast.22, bf16[2,60,8,384]{3,2,1,0:T(8,128)(2,1)} %bitcast.19, bf16[4,8,384]{2,1,0:T(8,128)(2,1)S(1)} %collective-permute-done.from_left_ref, ...), custom_call_target="tpu_custom_call" | custom-call | flops 2000000000 | bytes 6000000 | tf_op jit(solution)/shard_map/pack_rows/pallas_call | solution.py:411
  15.2 3.0 %collective-permute-start.3 = (bf16[4,64,384]{2,1,0:T(8,128)(2,1)S(1)}, bf16[4,64,384]{2,1,0:T(8,128)(2,1)S(1)}, u32[]{:S(2)}, u32[]{:S(2)}) collective-permute-start(bf16[4,64,384]{2,1,0:T(8,128)(2,1)S(1)} %get-tuple-element.29), channel_id=1, source_target_pairs={{0,4},{1,5},{2,6},{3,7},{4,8},{5,9},{6,10},{7,11},{8,12},{9,13},{1... | collective-permute-start | bytes 589832 | tf_op jit(solution)/shard_map/ppermute | solution.py:415
  18.2 2.5 %collective-permute-start.5 = (bf16[4,64,384]{2,1,0:T(8,128)(2,1)S(1)}, bf16[4,64,384]{2,1,0:T(8,128)(2,1)S(1)}, u32[]{:S(2)}, u32[]{:S(2)}) collective-permute-start(bf16[4,64,384]{2,1,0:T(8,128)(2,1)S(1)} %get-tuple-element.39), channel_id=1, source_target_pairs={{4,0},{5,1},{6,2},{7,3},{8,4},{9,5},{10,6},{11,7},{12,8},{13,9},{1... | collective-permute-start | bytes 589832 | tf_op jit(solution)/shard_map/ppermute | solution.py:416
  20.6 0.0 all-to-all-done.stat_ref
  20.6 0.0 copy-done
  20.6 0.0 copy-done.1
  20.6 9.6 %frame0.1 = (bf16[360,384]{1,0:T(8,128)(2,1)S(1)}, f32[2,60,384]{2,1,0:T(8,128)S(1)}, bf16[60,8,384]{2,1,0:T(8,128)(2,1)S(1)}, bf16[3,1152,1152]{2,1,0:T(8,128)(...) custom-call(f32[32,1,128]{2,1,0:T(1,128)S(1)} %all-to-all-done.stat_, ...), custom_call_target="tpu_custom_call" | custom-call | flops 10000000000 | bytes 30000000 | tf_op jit(solution)/shard_map/frame0/pallas_call | solution.py:418
  30.3 1.9 %collective-permute-start.2 = (bf16[360,384]{1,0:T(8,128)(2,1)S(1)}, bf16[360,384]{1,0:T(8,128)(2,1)S(1)}, u32[]{:S(2)}, u32[]{:S(2)}) collective-permute-start(bf16[360,384]{1,0:T(8,128)(2,1)S(1)} %get-tuple-element.27), channel_id=1, source_target_pairs={{0,32},{32,64},{64,96},{96,128},{128,160},{160,192},{192,224},{224... | collective-permute-start | bytes 829448 | tf_op jit(solution)/shard_map/ppermute | solution.py:425
  32.2 0.0 collective-permute-done.3.beyond_ref
  32.2 4.1 %frame1_first.1 = (bf16[300,384]{1,0:T(8,128)(2,1)S(1)}, bf16[60,8,384]{2,1,0:T(8,128)(2,1)S(1)}, bf16[10,64,1152]{2,1,0:T(8,128)(2,1)S(1)}) custom-call(bf16[2,60,8,384]{3,2,1,0:T(8,128)(2,1)S(1)} %get-tuple-element.28.x_ref, f32[4,8,384]{2,1,0:T(8,128)S(1)} %get-tuple-element.25.left_ref, f32[4,8,384]{2,1,0:T(8,128)S(1)} %get-tuple-element.26.right_ref, ...), custom_call_target="tpu_custom_call" | custom-call | flops 4000000000 | bytes 12000000 | tf_op jit(solution)/shard_map/frame1_first/pallas_call | solution.py:429
  36.3 1.7 %collective-permute-start.4 = (bf16[300,384]{1,0:T(8,128)(2,1)S(1)}, bf16[300,384]{1,0:T(8,128)(2,1)S(1)}, u32[]{:S(2)}, u32[]{:S(2)}) collective-permute-start(bf16[300,384]{1,0:T(8,128)(2,1)S(1)} %get-tuple-element.35), channel_id=1, source_target_pairs={{0,32},{32,64},{64,96},{96,128},{128,160},{160,192},{192,224},{224... | collective-permute-start | bytes 691208 | tf_op jit(solution)/shard_map/ppermute | solution.py:433
  38.0 0.0 collective-permute-done.5.beyond_ref
  38.0 3.8 %frame1_second.1 = bf16[300,384]{1,0:T(8,128)(2,1)S(1)} custom-call(bf16[2,60,8,384]{3,2,1,0:T(8,128)(2,1)S(1)} %get-tuple-element.28.x_ref, f32[4,8,384]{2,1,0:T(8,128)S(1)} %get-tuple-element.25.left_ref, f32[4,8,384]{2,1,0:T(8,128)S(1)} %get-tuple-element.26.right_ref, bf16[4,64,384]{2,1,0:T(8,128)(2,1)S(1)} %collective-permute-done.5.beyond_ref, ...), custom_call_target="tpu_custom_call" | custom-call | flops 4000000000 | bytes 12000000 | tf_op jit(solution)/shard_map/frame1_second/pallas_call | solution.py:434
  41.9 1.7 %collective-permute-start.6 = (bf16[300,384]{1,0:T(8,128)(2,1)S(1)}, bf16[300,384]{1,0:T(8,128)(2,1)S(1)}, u32[]{:S(2)}, u32[]{:S(2)}) collective-permute-start(bf16[300,384]{1,0:T(8,128)(2,1)S(1)} %frame1_second.1), channel_id=1, source_target_pairs={{0,32},{32,64},{64,96},{96,128},{128,160},{160,192},{192,224},{224... | collective-permute-start | bytes 691208 | tf_op jit(solution)/shard_map/ppermute | solution.py:437
  43.6 0.0 collective-permute-done.2.y0_ref
  43.6 3.9 %collective-permute-done.4.half_ref = bf16[300,384]{1,0:T(8,128)(2,1)S(1)} collective-permute-done((bf16[300,384]{1,0:T(8,128)(2,1)S(1)}, bf16[300,384]{1,0:T(8,128)(2,1)S(1)}, u32[]{:S(2)}, u32[]{:S(2)}) %collective-permute-start.4) | collective-permute-done | bytes 230432 | tf_op jit(solution)/shard_map/ppermute | solution.py:433
  47.5 1.0 %spread_rows.1 = (f32[2,3,480,128]{3,2,1,0:T(8,128)S(1)}, bf16[2,60,8,384]{3,2,1,0:T(8,128)(2,1)}) custom-call(bf16[360,384]{1,0:T(8,128)(2,1)S(1)} %collective-permute-done.2.y0_ref, bf16[300,384]{1,0:T(8,128)(2,1)S(1)} %collective-permute-done.4.half_ref, bf16[60,8,384]{2,1,0:T(8,128)(2,1)S(1)} %get-tuple-element.36.new0_ref, ...), custom_call_target="tpu_custom_call" | custom-call | flops 10000000000 | bytes 30000000 | tf_op jit(solution)/shard_map/spread_rows/pallas_call | solution.py:438
  48.5 4.0 %collective-permute-done.6.half_ref = bf16[300,384]{1,0:T(8,128)(2,1)S(1)} collective-permute-done((bf16[300,384]{1,0:T(8,128)(2,1)S(1)}, bf16[300,384]{1,0:T(8,128)(2,1)S(1)}, u32[]{:S(2)}, u32[]{:S(2)}) %collective-permute-start.6) | collective-permute-done | bytes 230432 | tf_op jit(solution)/shard_map/ppermute | solution.py:437
  52.5 1.1 %join_rows.1 = bf16[2,60,8,384]{3,2,1,0:T(8,128)(2,1)} custom-call(f32[2,3,480,128]{3,2,1,0:T(8,128)S(1)} %get-tuple-element.38.flat_ref, bf16[300,384]{1,0:T(8,128)(2,1)S(1)} %collective-permute-done.6.half_ref), custom_call_target="tpu_custom_call" | custom-call | flops 1000000000 | bytes 3000000 | tf_op jit(solution)/shard_map/join_rows/pallas_call | solution.py:442
Async XLA Ops:
  3.1 10.4 %collective-permute-start = (bf16[4,8,384]{2,1,0:T(8,128)(2,1)S(1)}, bf16[4,8,384]{2,1,0:T(8,128)(2,1)S(1)}, u32[]{:S(2)}, u32[]{:S(2)}) collective-permute-start(bf16[4,8,384]{2,1,0:T(8,128)(2,1)S(1)} %get-tuple-element.23), channel_id=1, source_target_pairs={{0,1},{1,2},{2,3},{3,0},{4,5},{5,6},{6,7},{7,4},{8,9},{9,10},{10,1... | collective-permute-start | bytes 73736 | tf_op jit(solution)/shard_map/ppermute | solution.py:409
  5.8 7.8 %collective-permute-start.1 = (bf16[4,8,384]{2,1,0:T(8,128)(2,1)S(1)}, bf16[4,8,384]{2,1,0:T(8,128)(2,1)S(1)}, u32[]{:S(2)}, u32[]{:S(2)}) collective-permute-start(bf16[4,8,384]{2,1,0:T(8,128)(2,1)S(1)} %get-tuple-element.24), channel_id=1, source_target_pairs={{1,0},{2,1},{3,2},{0,3},{5,4},{6,5},{7,6},{4,7},{9,8},{10,9},{11,1... | collective-permute-start | bytes 73736 | tf_op jit(solution)/shard_map/ppermute | solution.py:410
  6.5 14.1 %all-to-all-start = ((f32[32,1,128]{2,1,0:T(1,128)}), f32[32,1,128]{2,1,0:T(1,128)S(1)}, u32[]{:S(2)}, u32[]{:S(2)}) async-start(f32[32,1,128]{2,1,0:T(1,128)} %get-tuple-element.22), calls=%async_computation | async-start | bytes 32768 | tf_op jit(solution)/shard_map/all_to_all | solution.py:405
  13.5 7.1 %copy-start = (f32[1,384]{1,0:T(1,128)S(1)}, f32[1,384]{1,0:T(1,128)}, u32[]{:S(2)}) copy-start(f32[1,384]{1,0:T(1,128)} %gain_ref.1) | copy-start | bytes 4612
  13.5 7.1 %copy-start.1 = (f32[1,384]{1,0:T(1,128)S(1)}, f32[1,384]{1,0:T(1,128)}, u32[]{:S(2)}) copy-start(f32[1,384]{1,0:T(1,128)} %bias_ref.5) | copy-start | bytes 4612
  15.2 17.0 %collective-permute-start.3 = (bf16[4,64,384]{2,1,0:T(8,128)(2,1)S(1)}, bf16[4,64,384]{2,1,0:T(8,128)(2,1)S(1)}, u32[]{:S(2)}, u32[]{:S(2)}) collective-permute-start(bf16[4,64,384]{2,1,0:T(8,128)(2,1)S(1)} %get-tuple-element.29), channel_id=1, source_target_pairs={{0,4},{1,5},{2,6},{3,7},{4,8},{5,9},{6,10},{7,11},{8,12},{9,13},{1... | collective-permute-start | bytes 589832 | tf_op jit(solution)/shard_map/ppermute | solution.py:415
  18.2 19.9 %collective-permute-start.5 = (bf16[4,64,384]{2,1,0:T(8,128)(2,1)S(1)}, bf16[4,64,384]{2,1,0:T(8,128)(2,1)S(1)}, u32[]{:S(2)}, u32[]{:S(2)}) collective-permute-start(bf16[4,64,384]{2,1,0:T(8,128)(2,1)S(1)} %get-tuple-element.39), channel_id=1, source_target_pairs={{4,0},{5,1},{6,2},{7,3},{8,4},{9,5},{10,6},{11,7},{12,8},{13,9},{1... | collective-permute-start | bytes 589832 | tf_op jit(solution)/shard_map/ppermute | solution.py:416
  30.3 13.4 %collective-permute-start.2 = (bf16[360,384]{1,0:T(8,128)(2,1)S(1)}, bf16[360,384]{1,0:T(8,128)(2,1)S(1)}, u32[]{:S(2)}, u32[]{:S(2)}) collective-permute-start(bf16[360,384]{1,0:T(8,128)(2,1)S(1)} %get-tuple-element.27), channel_id=1, source_target_pairs={{0,32},{32,64},{64,96},{96,128},{128,160},{160,192},{192,224},{224... | collective-permute-start | bytes 829448 | tf_op jit(solution)/shard_map/ppermute | solution.py:425
  36.3 11.2 %collective-permute-start.4 = (bf16[300,384]{1,0:T(8,128)(2,1)S(1)}, bf16[300,384]{1,0:T(8,128)(2,1)S(1)}, u32[]{:S(2)}, u32[]{:S(2)}) collective-permute-start(bf16[300,384]{1,0:T(8,128)(2,1)S(1)} %get-tuple-element.35), channel_id=1, source_target_pairs={{0,32},{32,64},{64,96},{96,128},{128,160},{160,192},{192,224},{224... | collective-permute-start | bytes 691208 | tf_op jit(solution)/shard_map/ppermute | solution.py:433
  41.9 10.6 %collective-permute-start.6 = (bf16[300,384]{1,0:T(8,128)(2,1)S(1)}, bf16[300,384]{1,0:T(8,128)(2,1)S(1)}, u32[]{:S(2)}, u32[]{:S(2)}) collective-permute-start(bf16[300,384]{1,0:T(8,128)(2,1)S(1)} %frame1_second.1), channel_id=1, source_target_pairs={{0,32},{32,64},{64,96},{96,128},{128,160},{160,192},{192,224},{224... | collective-permute-start | bytes 691208 | tf_op jit(solution)/shard_map/ppermute | solution.py:437

commit v4 on v3

--- a/solution.py
+++ b/solution.py
@@ -164,15 +164,20 @@
     return lax.div(tile, TCOL), lax.rem(tile, TCOL)
 
 
-BLOCK = 4
-
-
-def wide_taps(taps_ref, first):
-    return jnp.concatenate([taps_ref[first + a : first + a + BLOCK].reshape(BLOCK * WP, -1) for a in range(3)], axis=1)
-
-
-def product(taps_ref, first, v_ref, at):
-    return jnp.dot(wide_taps(taps_ref, first), tap_weights(v_ref, at, at + 1), preferred_element_type=F32)
+EARLY = 5
+
+
+def wide_taps(taps_ref, first, count):
+    return jnp.concatenate([taps_ref[first + a : first + a + count].reshape(count * WP, -1) for a in range(3)], axis=1)
+
+
+def product(taps_ref, first, count, v_ref, at):
+    return jnp.dot(wide_taps(taps_ref, first, count), tap_weights(v_ref, at, at + 1), preferred_element_type=F32)
+
+
+def product_with(rim_taps_ref, rim, taps_ref, first, count, v_ref, at):
+    lhs = jnp.concatenate([wide_taps(taps_ref, first, count), wide_taps(rim_taps_ref, rim, 1)], axis=0)
+    return jnp.dot(lhs, tap_weights(v_ref, at, at + 1), preferred_element_type=F32)
 
 
 def tap_weights(v_ref, lo, hi):
@@ -223,19 +228,22 @@
     line_ref[at * value.shape[0] : (at + 1) * value.shape[0], :] = value
 
 
-def finish_rows(total, first, flat_ref, bias, width, rows, line_ref, rim_ref, skip=0):
-    for at in range(BLOCK):
+def finish_rows(total, first, count, flat_ref, bias, width, rows, line_ref, at_line):
+    rim = None
+    for at in range(count):
         r = first + at
         whole = get_row(flat_ref, r, rows, width) + bias + total[at * WP : at * WP + width]
         if r in (0, rows - 1):
-            rim_ref[r // (rows - 1)] = whole
+            rim = whole
         else:
-            put_cells(line_ref, r - 1 - skip, whole)
+            put_cells(line_ref, at_line, whole)
+            at_line += 1
+    return rim
 
 
 def frame0_kernel(tiles, stat_ref, c_hbm, x_hbm, left_ref, right_ref, w_hbm, gain_ref, bias_ref,
-                  y_ref, rim_ref, new_ref, v_ref, coef_ref, x_ref, x1_ref, xa_ref,
-                  c_ref, x0_ref, sum_ref, pad_ref, flat_ref, line_ref, frame_sems, sems):
+                  y_ref, new_ref, v_ref, coef_ref, x_ref, x0_ref, x1_ref, xa_ref,
+                  c_ref, sum_ref, pad_ref, flat_ref, line_ref, frame_sems, sems):
     _, width, rows, chans = x_ref.shape
     loads = [fetch(c_hbm, 0, c_ref.at[0], frame_sems.at[0]), fetch(c_hbm, 1, c_ref.at[1], frame_sems.at[1]),
              fetch(x_hbm, 0, x_ref.at[0], frame_sems.at[2])]
@@ -278,23 +286,24 @@
     wait_all(loads[2])
     frame_taps(0, x_ref, left_ref, right_ref, coef_ref[0:1], coef_ref[1:2], pad_ref, flat_ref, new_ref, xa_ref)
     put_lines(flat_ref, x_ref[0].astype(F32).reshape(width * rows, chans))
-    firsts = range(0, rows, BLOCK)
+    step = (rows - 2) // 2
+    firsts = (1, 1 + step)
     wait_weights(0)
     for first in firsts:
-        sum_ref[first * WP : (first + BLOCK) * WP] = product(x0_ref, first, v_ref, 2)
+        sum_ref[first * WP : (first + step) * WP] = product(x0_ref, first, step, v_ref, 2)
     wait_weights(1)
     for first in firsts:
-        sum_ref[first * WP : (first + BLOCK) * WP] += product(x1_ref, first, v_ref, 1)
+        sum_ref[first * WP : (first + step) * WP] += product(x1_ref, first, step, v_ref, 1)
     wait_weights(2)
     for first in firsts:
-        total = sum_ref[first * WP : (first + BLOCK) * WP] + product(xa_ref, first, v_ref, 0)
-        finish_rows(total, first, flat_ref, bias_ref[...], width, rows, line_ref, rim_ref)
+        total = sum_ref[first * WP : (first + step) * WP] + product(xa_ref, first, step, v_ref, 0)
+        finish_rows(total, first, step, flat_ref, bias_ref[...], width, rows, line_ref, first - 1)
     y_ref[...] = line_ref[...].astype(BF16)
     wait_all(loads[3])
 
 
-def edge_part(side, src_ref, v_ref, coef_ref, rim0_ref, rim1_ref, pad_ref, halo_ref):
-    _, width, chans = rim0_ref.shape
+def edge_part(side, src_ref, v_ref, coef_ref, rim0, rim1, pad_ref, halo_ref):
+    width, chans = rim0.shape
     row, col = tile_place()
     last = lax.div(lax.axis_size("tile"), TCOL) - 1
     inside = (row > 0) if side == 0 else (row < last)
@@ -316,23 +325,26 @@
              for k, (lo, hi) in enumerate(((2, 3), (1, 3), (0, 2), (0, 1)))]
     total0 = parts[0] + parts[1][:, :chans] + parts[2][:, :chans]
     total1 = parts[1][:, chans:] + parts[2][:, chans:] + parts[3]
-    return rim0_ref[side] + total0[:width], rim1_ref[side] + total1[:width]
-
-
-def half_kernel(side, x_ref, left_ref, right_ref, beyond_ref, v_ref, x1_ref, xa0_ref, coef_ref, bias_ref, rim0_ref, *refs):
+    return rim0 + total0[:width], rim1 + total1[:width]
+
+
+def half_kernel(side, x_ref, left_ref, right_ref, beyond_ref, v_ref, x0_ref, x1_ref, xa0_ref, coef_ref, bias_ref, *refs):
     if side == 0:
-        y_ref, new_ref, xa_ref, pad_ref, flat_ref, rim1_ref, halo_ref, line_ref = refs
+        y_ref, new_ref, xa_ref, pad_ref, flat_ref, halo_ref, line_ref = refs
         frame_taps(1, x_ref, left_ref, right_ref, coef_ref[2:3], coef_ref[3:4], pad_ref, flat_ref, new_ref, xa_ref)
     else:
-        xa_ref, y_ref, pad_ref, flat_ref, rim1_ref, halo_ref, line_ref = refs
+        xa_ref, y_ref, pad_ref, flat_ref, halo_ref, line_ref = refs
     _, width, rows, chans = x_ref.shape
+    first, count, rim = (EARLY, rows - EARLY, rows - 1) if side else (0, EARLY, 0)
+    total = (product_with(x0_ref, rim, x1_ref, first, count, v_ref, 2)
+             + product_with(x1_ref, rim, xa0_ref, first, count, v_ref, 1)
+             + product_with(xa0_ref, rim, xa_ref, first, count, v_ref, 0))
+    put_lines(flat_ref, x_ref[0].astype(F32).reshape(width * rows, chans))
+    rim0 = get_row(flat_ref, rim, rows, width) + bias_ref[...] + total[count * WP : count * WP + width]
     put_lines(flat_ref, x_ref[1].astype(F32).reshape(width * rows, chans))
-    first = side * BLOCK
-    total = (product(x1_ref, first, v_ref, 2) + product(xa0_ref, first, v_ref, 1)
-             + product(xa_ref, first, v_ref, 0))
-    finish_rows(total, first, flat_ref, bias_ref[...], width, rows, line_ref, rim1_ref, side * (BLOCK - 1))
-    for f, row in enumerate(edge_part(side, beyond_ref, v_ref, coef_ref, rim0_ref, rim1_ref, pad_ref, halo_ref)):
-        put_cells(line_ref, BLOCK - 1 + f, row)
+    rim1 = finish_rows(total, first, count, flat_ref, bias_ref[...], width, rows, line_ref, 0)
+    for f, row in enumerate(edge_part(side, beyond_ref, v_ref, coef_ref, rim0, rim1, pad_ref, halo_ref)):
+        put_cells(line_ref, count - 1 + f, row)
     y_ref[...] = line_ref[...].astype(BF16)
 
 
@@ -344,8 +356,8 @@
     for r in range(rows - 2):
         put_row(flat_ref.at[0], r + 1, rows, width, y0[r * width : (r + 1) * width])
     for f in range(2):
-        put_row(flat_ref.at[f], 0, rows, width, half[(BLOCK - 1 + f) * width : (BLOCK + f) * width])
-    for at in range(BLOCK - 1):
+        put_row(flat_ref.at[f], 0, rows, width, half[(EARLY - 1 + f) * width : (EARLY + f) * width])
+    for at in range(EARLY - 1):
         put_row(flat_ref.at[1], at + 1, rows, width, half[at * width : (at + 1) * width])
 
 
@@ -353,12 +365,13 @@
     _, width, rows, chans = out_ref.shape
     line = lax.broadcasted_iota(jnp.int32, (width * rows, LANES), 0) & (rows - 1)
     half = half_ref[...].astype(F32)
+    late_rows = rows - EARLY
     copies = []
-    for f, late in ((0, line == rows - 1), (1, line >= rows - BLOCK)):
-        put_row(scr_ref.at[f], rows - 1, rows, width, half[(BLOCK - 1 + f) * width : (BLOCK + f) * width])
+    for f, late in ((0, line == rows - 1), (1, line >= rows - late_rows)):
+        put_row(scr_ref.at[f], rows - 1, rows, width, half[(late_rows - 1 + f) * width : (late_rows + f) * width])
         if f == 1:
-            for at in range(BLOCK - 1):
-                put_row(scr_ref.at[1], rows - BLOCK + at, rows, width, half[at * width : (at + 1) * width])
+            for at in range(late_rows - 1):
+                put_row(scr_ref.at[1], rows - late_rows + at, rows, width, half[at * width : (at + 1) * width])
         for j in range(flat_ref.shape[1]):
             whole = jnp.where(late, scr_ref[f, j], flat_ref[f, j])
             out_ref[f, :, :, j * LANES : (j + 1) * LANES] = whole.astype(BF16).reshape(width, rows, LANES)
@@ -390,7 +403,6 @@
     both = pltpu.VMEM((frames, width, rows, chans), BF16)
     pad = pltpu.VMEM((rows, 80, chans), F32)
     flat = pltpu.VMEM((chans // LANES, width * rows, LANES), F32)
-    rim = pltpu.VMEM((2, width, chans), F32)
     edge_rows = sds((4, WP, chans), BF16)
 
     def call(body, name, us, in_specs, out_specs, out_shape, scratch, aliases={}):
@@ -415,25 +427,26 @@
     above = lax.ppermute(bottom, "tile", next_row)
     below = lax.ppermute(top, "tile", back(next_row))
     onward = [(i, (i + 1) % sections) for i in range(sections)]
-    y0, rim0, new0, v, coef, xv, x1, xa0 = call(
+    y0, new0, v, coef, xv, x0, x1, xa0 = call(
         functools.partial(frame0_kernel, tiles), "frame0", 10, [VMEM, HBM, HBM, VMEM, VMEM, HBM, VMEM, VMEM], [VMEM] * 8,
-        (sds((inner * width, chans), BF16), rim, frame, pltpu.VMEM((3, 3 * chans, 3 * chans), BF16),
-         pltpu.VMEM((8, chans), F32), both, taps, taps),
-        [both, taps, pltpu.VMEM(acc, F32), pad, flat, pltpu.VMEM((inner * width, chans), F32),
+        (sds((inner * width, chans), BF16), frame, pltpu.VMEM((3, 3 * chans, 3 * chans), BF16),
+         pltpu.VMEM((8, chans), F32), both, taps, taps, taps),
+        [both, pltpu.VMEM(acc, F32), pad, flat, pltpu.VMEM((inner * width, chans), F32),
          DMA((4, PARTS)), DMA((3, 3))],
     )(stats, c, x, left, right, weights, gain, conv_bias)
     y0 = lax.ppermute(y0, "section", onward)
-    half = sds(((BLOCK + 1) * width, chans), BF16)
-    lines = pltpu.VMEM(((BLOCK + 1) * width, chans), F32)
+    early = ((EARLY + 1) * width, chans)
+    later = ((rows - EARLY + 1) * width, chans)
     halo = pltpu.VMEM((4, WP, 3 * chans), BF16)
     half_a, new1, xa1 = call(
-        functools.partial(half_kernel, 0), "frame1_first", 4, [VMEM] * 10, [VMEM] * 3, (half, frame, taps),
-        [pad, flat, rim, halo, lines],
-    )(xv, left, right, above, v, x1, xa0, coef, conv_bias, rim0)
+        functools.partial(half_kernel, 0), "frame1_first", 4, [VMEM] * 10, [VMEM] * 3, (sds(early, BF16), frame, taps),
+        [pad, flat, halo, pltpu.VMEM(early, F32)],
+    )(xv, left, right, above, v, x0, x1, xa0, coef, conv_bias)
     half_a = lax.ppermute(half_a, "section", onward)
     half_b = call(
-        functools.partial(half_kernel, 1), "frame1_second", 4, [VMEM] * 11, VMEM, half, [pad, flat, rim, halo, lines],
-    )(xv, left, right, below, v, x1, xa0, coef, conv_bias, rim0, xa1)
+        functools.partial(half_kernel, 1), "frame1_second", 4, [VMEM] * 11, VMEM, sds(later, BF16),
+        [pad, flat, halo, pltpu.VMEM(later, F32)],
+    )(xv, left, right, below, v, x0, x1, xa0, coef, conv_bias, xa1)
     half_b = lax.ppermute(half_b, "section", onward)
     spread, new = call(
         spread_kernel, "spread_rows", 10, [VMEM] * 4, [VMEM] * 2,

time: 54.1 us -> 52.4 us (0.969)
  waiting for transfers between devices: 7.9 us -> 6.05 us
    pallas_call x1, Pallas kernels: 4.13 us -> 5.73 us  [on_device(): call(functools.partial(half_kernel, 0), 'frame1_first', 4, [VMEM] * 10, [...]
    pallas_call x1, Pallas kernels: 9.6 us -> 8.35 us  [on_device(): call(functools.partial(frame0_kernel, tiles), 'frame0', 10, [VMEM, HBM, H...]
    ppermute x1, waiting for transfers between devices: 3.98 us -> 2.92 us  [on_device(): half_b = lax.ppermute(half_b, 'section', onward)]
    ppermute x1, waiting for transfers between devices: 3.9 us -> 3.12 us  [on_device(): half_a = lax.ppermute(half_a, 'section', onward)]
  transfers between devices with their start and end apart: 8 -> 8, of which waited for: 2 -> 2; matrix products, arithmetic and copies ran while one was open for 0% -> 0% of each run, Pallas kernels for 38% -> 40%
where the time goes in v4:
time: 52.4 us; the launch traced here: 52.2 us
  Pallas kernels  24.3 us (46%)
  starting transfers between devices  21 us (40%)
  waiting for transfers between devices  6.05 us (12%)
  between operations  0.87 us (2%)
    pallas_call x1, Pallas kernels, on_device(): call(functools.partial(frame0_kernel, tiles), 'frame0', 10, [VMEM, HBM, H...  8.35 us
    all_to_all x1, starting transfers between devices, on_device(): stats = lax.all_to_all(stat, 'tile', 0, 0, tiled=True)  7.01 us
    pallas_call x1, Pallas kernels, on_device(): call(functools.partial(half_kernel, 0), 'frame1_first', 4, [VMEM] * 10, [...  5.73 us
    pallas_call x1, Pallas kernels, on_device(): call(functools.partial(half_kernel, 1), 'frame1_second', 4, [VMEM] * 11,...  3.94 us
    ppermute x1, waiting for transfers between devices, on_device(): half_a = lax.ppermute(half_a, 'section', onward)  3.12 us
    ppermute x1, starting transfers between devices, on_device(): above = lax.ppermute(bottom, 'tile', next_row)  2.97 us
    ppermute x1, waiting for transfers between devices, on_device(): half_b = lax.ppermute(half_b, 'section', onward)  2.92 us
    ppermute x1, starting transfers between devices, on_device(): from_left = lax.ppermute(last_col, 'tile', next_col)  2.68 us
  transfers between devices with their start and end apart: 8, of which 2 were waited for; matrix products, arithmetic and copies ran while one was open for 0% of the time, Pallas kernels for 40%

profile of v4, /device:TPU:1, one launch (start us, length us, event | category | flops | bytes accessed | tf_op | source)
XLA Modules:
  0.0 52.2 jit_solution(9595500444674625541)
XLA Ops:
  0.6 2.5 %local_stats.1 = (f32[32,1,128]{2,1,0:T(1,128)}, bf16[4,8,384]{2,1,0:T(8,128)(2,1)S(1)}, bf16[4,8,384]{2,1,0:T(8,128)(2,1)S(1)}) custom-call(bf16[2,60,8,384]{3,2,1,0:T(8,128)(2,1)} %bitcast.18, bf16[2,60,8,384]{3,2,1,0:T(8,128)(2,1)} %bitcast.21), custom_call_target="tpu_custom_call" | custom-call | flops 1000000000 | bytes 3000000 | tf_op jit(solution)/shard_map/local_stats/pallas_call | solution.py:412
  3.1 2.7 %collective-permute-start = (bf16[4,8,384]{2,1,0:T(8,128)(2,1)S(1)}, bf16[4,8,384]{2,1,0:T(8,128)(2,1)S(1)}, u32[]{:S(2)}, u32[]{:S(2)}) collective-permute-start(bf16[4,8,384]{2,1,0:T(8,128)(2,1)S(1)} %get-tuple-element.23), channel_id=1, source_target_pairs={{0,1},{1,2},{2,3},{3,0},{4,5},{5,6},{6,7},{7,4},{8,9},{9,10},{10,1... | collective-permute-start | bytes 73736 | tf_op jit(solution)/shard_map/ppermute | solution.py:421
  5.8 0.7 %collective-permute-start.1 = (bf16[4,8,384]{2,1,0:T(8,128)(2,1)S(1)}, bf16[4,8,384]{2,1,0:T(8,128)(2,1)S(1)}, u32[]{:S(2)}, u32[]{:S(2)}) collective-permute-start(bf16[4,8,384]{2,1,0:T(8,128)(2,1)S(1)} %get-tuple-element.24), channel_id=1, source_target_pairs={{1,0},{2,1},{3,2},{0,3},{5,4},{6,5},{7,6},{4,7},{9,8},{10,9},{11,1... | collective-permute-start | bytes 73736 | tf_op jit(solution)/shard_map/ppermute | solution.py:422
  6.5 7.0 %all-to-all-start = ((f32[32,1,128]{2,1,0:T(1,128)}), f32[32,1,128]{2,1,0:T(1,128)S(1)}, u32[]{:S(2)}, u32[]{:S(2)}) async-start(f32[32,1,128]{2,1,0:T(1,128)} %get-tuple-element.22), calls=%async_computation | async-start | bytes 32768 | tf_op jit(solution)/shard_map/all_to_all | solution.py:417
  13.5 0.0 copy-start
  13.5 0.0 copy-start.1
  13.5 0.0 collective-permute-done.from_left_ref
  13.6 0.0 collective-permute-done.1.from_right_ref
  13.6 1.6 %pack_rows.1 = (bf16[4,64,384]{2,1,0:T(8,128)(2,1)S(1)}, bf16[4,64,384]{2,1,0:T(8,128)(2,1)S(1)}, f32[4,8,384]{2,1,0:T(8,128)S(1)}, f32[4,8,384]{2,1,0:T(8,128)S(1)}) custom-call(bf16[2,60,8,384]{3,2,1,0:T(8,128)(2,1)} %bitcast.22, bf16[2,60,8,384]{3,2,1,0:T(8,128)(2,1)} %bitcast.19, bf16[4,8,384]{2,1,0:T(8,128)(2,1)S(1)} %collective-permute-done.from_left_ref, ...), custom_call_target="tpu_custom_call" | custom-call | flops 2000000000 | bytes 6000000 | tf_op jit(solution)/shard_map/pack_rows/pallas_call | solution.py:423
  15.2 3.0 %collective-permute-start.3 = (bf16[4,64,384]{2,1,0:T(8,128)(2,1)S(1)}, bf16[4,64,384]{2,1,0:T(8,128)(2,1)S(1)}, u32[]{:S(2)}, u32[]{:S(2)}) collective-permute-start(bf16[4,64,384]{2,1,0:T(8,128)(2,1)S(1)} %get-tuple-element.29), channel_id=1, source_target_pairs={{0,4},{1,5},{2,6},{3,7},{4,8},{5,9},{6,10},{7,11},{8,12},{9,13},{1... | collective-permute-start | bytes 589832 | tf_op jit(solution)/shard_map/ppermute | solution.py:427
  18.2 2.3 %collective-permute-start.5 = (bf16[4,64,384]{2,1,0:T(8,128)(2,1)S(1)}, bf16[4,64,384]{2,1,0:T(8,128)(2,1)S(1)}, u32[]{:S(2)}, u32[]{:S(2)}) collective-permute-start(bf16[4,64,384]{2,1,0:T(8,128)(2,1)S(1)} %get-tuple-element.39), channel_id=1, source_target_pairs={{4,0},{5,1},{6,2},{7,3},{8,4},{9,5},{10,6},{11,7},{12,8},{13,9},{1... | collective-permute-start | bytes 589832 | tf_op jit(solution)/shard_map/ppermute | solution.py:428
  20.5 0.0 all-to-all-done.stat_ref
  20.5 0.0 copy-done
  20.5 0.0 copy-done.1
  20.5 8.3 %frame0.1 = (bf16[360,384]{1,0:T(8,128)(2,1)S(1)}, bf16[60,8,384]{2,1,0:T(8,128)(2,1)S(1)}, bf16[3,1152,1152]{2,1,0:T(8,128)(2,1)S(1)}, f32[8,384]{1,0:T(8,128)S...) custom-call(f32[32,1,128]{2,1,0:T(1,128)S(1)} %all-to-all-done.stat_, ...), custom_call_target="tpu_custom_call" | custom-call | flops 10000000000 | bytes 30000000 | tf_op jit(solution)/shard_map/frame0/pallas_call | solution.py:430
  28.8 1.9 %collective-permute-start.2 = (bf16[360,384]{1,0:T(8,128)(2,1)S(1)}, bf16[360,384]{1,0:T(8,128)(2,1)S(1)}, u32[]{:S(2)}, u32[]{:S(2)}) collective-permute-start(bf16[360,384]{1,0:T(8,128)(2,1)S(1)} %get-tuple-element.27), channel_id=1, source_target_pairs={{0,32},{32,64},{64,96},{96,128},{128,160},{160,192},{192,224},{224... | collective-permute-start | bytes 829448 | tf_op jit(solution)/shard_map/ppermute | solution.py:437
  30.7 0.0 collective-permute-done.3.beyond_ref
  30.7 5.7 %frame1_first.1 = (bf16[360,384]{1,0:T(8,128)(2,1)S(1)}, bf16[60,8,384]{2,1,0:T(8,128)(2,1)S(1)}, bf16[10,64,1152]{2,1,0:T(8,128)(2,1)S(1)}) custom-call(bf16[2,60,8,384]{3,2,1,0:T(8,128)(2,1)S(1)} %get-tuple-element.28.x_ref, f32[4,8,384]{2,1,0:T(8,128)S(1)} %get-tuple-element.25.left_ref, f32[4,8,384]{2,1,0:T(8,128)S(1)} %get-tuple-element.26.right_ref, ...), custom_call_target="tpu_custom_call" | custom-call | flops 4000000000 | bytes 12000000 | tf_op jit(solution)/shard_map/frame1_first/pallas_call | solution.py:441
  36.4 1.7 %collective-permute-start.4 = (bf16[360,384]{1,0:T(8,128)(2,1)S(1)}, bf16[360,384]{1,0:T(8,128)(2,1)S(1)}, u32[]{:S(2)}, u32[]{:S(2)}) collective-permute-start(bf16[360,384]{1,0:T(8,128)(2,1)S(1)} %get-tuple-element.35), channel_id=1, source_target_pairs={{0,32},{32,64},{64,96},{96,128},{128,160},{160,192},{192,224},{224... | collective-permute-start | bytes 829448 | tf_op jit(solution)/shard_map/ppermute | solution.py:445
  38.2 0.0 collective-permute-done.5.beyond_ref
  38.2 3.9 %frame1_second.1 = bf16[240,384]{1,0:T(8,128)(2,1)S(1)} custom-call(bf16[2,60,8,384]{3,2,1,0:T(8,128)(2,1)S(1)} %get-tuple-element.28.x_ref, f32[4,8,384]{2,1,0:T(8,128)S(1)} %get-tuple-element.25.left_ref, f32[4,8,384]{2,1,0:T(8,128)S(1)} %get-tuple-element.26.right_ref, bf16[4,64,384]{2,1,0:T(8,128)(2,1)S(1)} %collective-permute-done.5.beyond_ref, ...), custom_call_target="tpu_custom_call" | custom-call | flops 4000000000 | bytes 12000000 | tf_op jit(solution)/shard_map/frame1_second/pallas_call | solution.py:446
  42.1 1.7 %collective-permute-start.6 = (bf16[240,384]{1,0:T(8,128)(2,1)S(1)}, bf16[240,384]{1,0:T(8,128)(2,1)S(1)}, u32[]{:S(2)}, u32[]{:S(2)}) collective-permute-start(bf16[240,384]{1,0:T(8,128)(2,1)S(1)} %frame1_second.1), channel_id=1, source_target_pairs={{0,32},{32,64},{64,96},{96,128},{128,160},{160,192},{192,224},{224... | collective-permute-start | bytes 552968 | tf_op jit(solution)/shard_map/ppermute | solution.py:450
  43.8 0.0 collective-permute-done.2.y0_ref
  43.8 3.1 %collective-permute-done.4.half_ref = bf16[360,384]{1,0:T(8,128)(2,1)S(1)} collective-permute-done((bf16[360,384]{1,0:T(8,128)(2,1)S(1)}, bf16[360,384]{1,0:T(8,128)(2,1)S(1)}, u32[]{:S(2)}, u32[]{:S(2)}) %collective-permute-start.4) | collective-permute-done | bytes 276512 | tf_op jit(solution)/shard_map/ppermute | solution.py:445
  47.0 1.0 %spread_rows.1 = (f32[2,3,480,128]{3,2,1,0:T(8,128)S(1)}, bf16[2,60,8,384]{3,2,1,0:T(8,128)(2,1)}) custom-call(bf16[360,384]{1,0:T(8,128)(2,1)S(1)} %collective-permute-done.2.y0_ref, bf16[360,384]{1,0:T(8,128)(2,1)S(1)} %collective-permute-done.4.half_ref, bf16[60,8,384]{2,1,0:T(8,128)(2,1)S(1)} %get-tuple-element.36.new0_ref, ...), custom_call_target="tpu_custom_call" | custom-call | flops 10000000000 | bytes 30000000 | tf_op jit(solution)/shard_map/spread_rows/pallas_call | solution.py:451
  48.0 2.9 %collective-permute-done.6.half_ref = bf16[240,384]{1,0:T(8,128)(2,1)S(1)} collective-permute-done((bf16[240,384]{1,0:T(8,128)(2,1)S(1)}, bf16[240,384]{1,0:T(8,128)(2,1)S(1)}, u32[]{:S(2)}, u32[]{:S(2)}) %collective-permute-start.6) | collective-permute-done | bytes 184352 | tf_op jit(solution)/shard_map/ppermute | solution.py:450
  50.9 1.1 %join_rows.1 = bf16[2,60,8,384]{3,2,1,0:T(8,128)(2,1)} custom-call(f32[2,3,480,128]{3,2,1,0:T(8,128)S(1)} %get-tuple-element.38.flat_ref, bf16[240,384]{1,0:T(8,128)(2,1)S(1)} %collective-permute-done.6.half_ref), custom_call_target="tpu_custom_call" | custom-call | flops 1000000000 | bytes 3000000 | tf_op jit(solution)/shard_map/join_rows/pallas_call | solution.py:455
Async XLA Ops:
  3.1 10.4 %collective-permute-start = (bf16[4,8,384]{2,1,0:T(8,128)(2,1)S(1)}, bf16[4,8,384]{2,1,0:T(8,128)(2,1)S(1)}, u32[]{:S(2)}, u32[]{:S(2)}) collective-permute-start(bf16[4,8,384]{2,1,0:T(8,128)(2,1)S(1)} %get-tuple-element.23), channel_id=1, source_target_pairs={{0,1},{1,2},{2,3},{3,0},{4,5},{5,6},{6,7},{7,4},{8,9},{9,10},{10,1... | collective-permute-start | bytes 73736 | tf_op jit(solution)/shard_map/ppermute | solution.py:421
  5.8 7.8 %collective-permute-start.1 = (bf16[4,8,384]{2,1,0:T(8,128)(2,1)S(1)}, bf16[4,8,384]{2,1,0:T(8,128)(2,1)S(1)}, u32[]{:S(2)}, u32[]{:S(2)}) collective-permute-start(bf16[4,8,384]{2,1,0:T(8,128)(2,1)S(1)} %get-tuple-element.24), channel_id=1, source_target_pairs={{1,0},{2,1},{3,2},{0,3},{5,4},{6,5},{7,6},{4,7},{9,8},{10,9},{11,1... | collective-permute-start | bytes 73736 | tf_op jit(solution)/shard_map/ppermute | solution.py:422
  6.5 13.9 %all-to-all-start = ((f32[32,1,128]{2,1,0:T(1,128)}), f32[32,1,128]{2,1,0:T(1,128)S(1)}, u32[]{:S(2)}, u32[]{:S(2)}) async-start(f32[32,1,128]{2,1,0:T(1,128)} %get-tuple-element.22), calls=%async_computation | async-start | bytes 32768 | tf_op jit(solution)/shard_map/all_to_all | solution.py:417
  13.5 6.9 %copy-start = (f32[1,384]{1,0:T(1,128)S(1)}, f32[1,384]{1,0:T(1,128)}, u32[]{:S(2)}) copy-start(f32[1,384]{1,0:T(1,128)} %bias_ref.5) | copy-start | bytes 4612
  13.5 6.9 %copy-start.1 = (f32[1,384]{1,0:T(1,128)S(1)}, f32[1,384]{1,0:T(1,128)}, u32[]{:S(2)}) copy-start(f32[1,384]{1,0:T(1,128)} %gain_ref.1) | copy-start | bytes 4612
  15.2 15.5 %collective-permute-start.3 = (bf16[4,64,384]{2,1,0:T(8,128)(2,1)S(1)}, bf16[4,64,384]{2,1,0:T(8,128)(2,1)S(1)}, u32[]{:S(2)}, u32[]{:S(2)}) collective-permute-start(bf16[4,64,384]{2,1,0:T(8,128)(2,1)S(1)} %get-tuple-element.29), channel_id=1, source_target_pairs={{0,4},{1,5},{2,6},{3,7},{4,8},{5,9},{6,10},{7,11},{8,12},{9,13},{1... | collective-permute-start | bytes 589832 | tf_op jit(solution)/shard_map/ppermute | solution.py:427
  18.2 20.0 %collective-permute-start.5 = (bf16[4,64,384]{2,1,0:T(8,128)(2,1)S(1)}, bf16[4,64,384]{2,1,0:T(8,128)(2,1)S(1)}, u32[]{:S(2)}, u32[]{:S(2)}) collective-permute-start(bf16[4,64,384]{2,1,0:T(8,128)(2,1)S(1)} %get-tuple-element.39), channel_id=1, source_target_pairs={{4,0},{5,1},{6,2},{7,3},{8,4},{9,5},{10,6},{11,7},{12,8},{13,9},{1... | collective-permute-start | bytes 589832 | tf_op jit(solution)/shard_map/ppermute | solution.py:428
  28.8 15.0 %collective-permute-start.2 = (bf16[360,384]{1,0:T(8,128)(2,1)S(1)}, bf16[360,384]{1,0:T(8,128)(2,1)S(1)}, u32[]{:S(2)}, u32[]{:S(2)}) collective-permute-start(bf16[360,384]{1,0:T(8,128)(2,1)S(1)} %get-tuple-element.27), channel_id=1, source_target_pairs={{0,32},{32,64},{64,96},{96,128},{128,160},{160,192},{192,224},{224... | collective-permute-start | bytes 829448 | tf_op jit(solution)/shard_map/ppermute | solution.py:437
  36.4 10.5 %collective-permute-start.4 = (bf16[360,384]{1,0:T(8,128)(2,1)S(1)}, bf16[360,384]{1,0:T(8,128)(2,1)S(1)}, u32[]{:S(2)}, u32[]{:S(2)}) collective-permute-start(bf16[360,384]{1,0:T(8,128)(2,1)S(1)} %get-tuple-element.35), channel_id=1, source_target_pairs={{0,32},{32,64},{64,96},{96,128},{128,160},{160,192},{192,224},{224... | collective-permute-start | bytes 829448 | tf_op jit(solution)/shard_map/ppermute | solution.py:445
  42.1 8.8 %collective-permute-start.6 = (bf16[240,384]{1,0:T(8,128)(2,1)S(1)}, bf16[240,384]{1,0:T(8,128)(2,1)S(1)}, u32[]{:S(2)}, u32[]{:S(2)}) collective-permute-start(bf16[240,384]{1,0:T(8,128)(2,1)S(1)} %frame1_second.1), channel_id=1, source_target_pairs={{0,32},{32,64},{64,96},{96,128},{128,160},{160,192},{192,224},{224... | collective-permute-start | bytes 552968 | tf_op jit(solution)/shard_map/ppermute | solution.py:450

commit v5 on v4

--- a/solution.py
+++ b/solution.py
@@ -66,13 +66,14 @@
     return jnp.where(hit, 1.0, 0.0).astype(BF16)
 
 
-PARTS = 4
+PARTS = 12
 
 
 def fetch(hbm_ref, f, vmem_ref, sems):
-    step = hbm_ref.shape[1] // PARTS
+    parts = sems.shape[0]
+    step = hbm_ref.shape[1] // parts
     copies = [pltpu.make_async_copy(hbm_ref.at[f, pl.ds(p * step, step)], vmem_ref.at[pl.ds(p * step, step)],
-                                    sems.at[p]) for p in range(PARTS)]
+                                    sems.at[p]) for p in range(parts)]
     for copy in copies:
         copy.start()
     return copies
@@ -412,7 +413,7 @@
     stat, first_col, last_col = call(
         first_kernel, "local_stats", 1, [HBM] * 2, [VMEM] * 3,
         (sds((tiles, 1, 128), F32), sds((4, rows, chans), BF16), sds((4, rows, chans), BF16)),
-        [both, pltpu.VMEM((2, 2, rows, chans), BF16), DMA((2, PARTS)), DMA((2, 2))],
+        [both, pltpu.VMEM((2, 2, rows, chans), BF16), DMA((2, 1)), DMA((2, 2))],
     )(x, c)
     stats = lax.all_to_all(stat, "tile", 0, 0, tiled=True)
     next_col = [(i, i - i % TCOL + (i + 1) % TCOL) for i in range(tiles)]
@@ -422,7 +423,7 @@
     from_right = lax.ppermute(first_col, "tile", back(next_col))
     bottom, top, left, right = call(
         rows_kernel, "pack_rows", 2, [HBM, HBM, VMEM, VMEM], [VMEM] * 4, (edge_rows, edge_rows, cols, cols),
-        [pltpu.VMEM((4, width, rows, chans), BF16), flat, DMA((4, PARTS))],
+        [pltpu.VMEM((4, width, rows, chans), BF16), flat, DMA((4, 1))],
     )(c, x, from_left, from_right)
     above = lax.ppermute(bottom, "tile", next_row)
     below = lax.ppermute(top, "tile", back(next_row))

time: 52.4 us -> 52.3 us (level)
  transfers between devices with their start and end apart: 8 -> 8, of which waited for: 2 -> 3; matrix products, arithmetic and copies ran while one was open for 0% -> 0% of each run, Pallas kernels for 40% -> 39%
where the time goes in v5:
time: 52.3 us; the launch traced here: 52.1 us
  Pallas kernels  24 us (46%)
  starting transfers between devices  21 us (40%)
  waiting for transfers between devices  6.24 us (12%)
  between operations  0.87 us (2%)
    pallas_call x1, Pallas kernels, on_device(): call(functools.partial(frame0_kernel, tiles), 'frame0', 10, [VMEM, HBM, H...  8.34 us
    all_to_all x1, starting transfers between devices, on_device(): stats = lax.all_to_all(stat, 'tile', 0, 0, tiled=True)  7.01 us
    pallas_call x1, Pallas kernels, on_device(): call(functools.partial(half_kernel, 0), 'frame1_first', 4, [VMEM] * 10, [...  5.73 us
    pallas_call x1, Pallas kernels, on_device(): call(functools.partial(half_kernel, 1), 'frame1_second', 4, [VMEM] * 11,...  3.95 us
    ppermute x1, waiting for transfers between devices, on_device(): half_a = lax.ppermute(half_a, 'section', onward)  3.18 us
    ppermute x1, starting transfers between devices, on_device(): above = lax.ppermute(bottom, 'tile', next_row)  2.97 us
    ppermute x1, waiting for transfers between devices, on_device(): half_b = lax.ppermute(half_b, 'section', onward)  2.92 us
    ppermute x1, starting transfers between devices, on_device(): from_left = lax.ppermute(last_col, 'tile', next_col)  2.68 us
  transfers between devices with their start and end apart: 8, of which 3 were waited for; matrix products, arithmetic and copies ran while one was open for 0% of the time, Pallas kernels for 39%

profile of v5, /device:TPU:1, one launch (start us, length us, event | category | flops | bytes accessed | tf_op | source)
XLA Modules:
  0.0 52.1 jit_solution(6755164556710757677)
XLA Ops:
  0.6 2.4 %local_stats.1 = (f32[32,1,128]{2,1,0:T(1,128)}, bf16[4,8,384]{2,1,0:T(8,128)(2,1)S(1)}, bf16[4,8,384]{2,1,0:T(8,128)(2,1)S(1)}) custom-call(bf16[2,60,8,384]{3,2,1,0:T(8,128)(2,1)} %bitcast.18, bf16[2,60,8,384]{3,2,1,0:T(8,128)(2,1)} %bitcast.21), custom_call_target="tpu_custom_call" | custom-call | flops 1000000000 | bytes 3000000 | tf_op jit(solution)/shard_map/local_stats/pallas_call | solution.py:413
  3.0 2.7 %collective-permute-start = (bf16[4,8,384]{2,1,0:T(8,128)(2,1)S(1)}, bf16[4,8,384]{2,1,0:T(8,128)(2,1)S(1)}, u32[]{:S(2)}, u32[]{:S(2)}) collective-permute-start(bf16[4,8,384]{2,1,0:T(8,128)(2,1)S(1)} %get-tuple-element.23), channel_id=1, source_target_pairs={{0,1},{1,2},{2,3},{3,0},{4,5},{5,6},{6,7},{7,4},{8,9},{9,10},{10,1... | collective-permute-start | bytes 73736 | tf_op jit(solution)/shard_map/ppermute | solution.py:422
  5.7 0.7 %collective-permute-start.1 = (bf16[4,8,384]{2,1,0:T(8,128)(2,1)S(1)}, bf16[4,8,384]{2,1,0:T(8,128)(2,1)S(1)}, u32[]{:S(2)}, u32[]{:S(2)}) collective-permute-start(bf16[4,8,384]{2,1,0:T(8,128)(2,1)S(1)} %get-tuple-element.24), channel_id=1, source_target_pairs={{1,0},{2,1},{3,2},{0,3},{5,4},{6,5},{7,6},{4,7},{9,8},{10,9},{11,1... | collective-permute-start | bytes 73736 | tf_op jit(solution)/shard_map/ppermute | solution.py:423
  6.4 7.0 %all-to-all-start = ((f32[32,1,128]{2,1,0:T(1,128)}), f32[32,1,128]{2,1,0:T(1,128)S(1)}, u32[]{:S(2)}, u32[]{:S(2)}) async-start(f32[32,1,128]{2,1,0:T(1,128)} %get-tuple-element.22), calls=%async_computation | async-start | bytes 32768 | tf_op jit(solution)/shard_map/all_to_all | solution.py:418
  13.4 0.0 copy-start
  13.4 0.0 copy-start.1
  13.5 0.0 collective-permute-done.from_left_ref
  13.5 0.0 collective-permute-done.1.from_right_ref
  13.5 1.4 %pack_rows.1 = (bf16[4,64,384]{2,1,0:T(8,128)(2,1)S(1)}, bf16[4,64,384]{2,1,0:T(8,128)(2,1)S(1)}, f32[4,8,384]{2,1,0:T(8,128)S(1)}, f32[4,8,384]{2,1,0:T(8,128)S(1)}) custom-call(bf16[2,60,8,384]{3,2,1,0:T(8,128)(2,1)} %bitcast.22, bf16[2,60,8,384]{3,2,1,0:T(8,128)(2,1)} %bitcast.19, bf16[4,8,384]{2,1,0:T(8,128)(2,1)S(1)} %collective-permute-done.from_left_ref, ...), custom_call_target="tpu_custom_call" | custom-call | flops 2000000000 | bytes 6000000 | tf_op jit(solution)/shard_map/pack_rows/pallas_call | solution.py:424
  14.9 3.0 %collective-permute-start.3 = (bf16[4,64,384]{2,1,0:T(8,128)(2,1)S(1)}, bf16[4,64,384]{2,1,0:T(8,128)(2,1)S(1)}, u32[]{:S(2)}, u32[]{:S(2)}) collective-permute-start(bf16[4,64,384]{2,1,0:T(8,128)(2,1)S(1)} %get-tuple-element.29), channel_id=1, source_target_pairs={{0,4},{1,5},{2,6},{3,7},{4,8},{5,9},{6,10},{7,11},{8,12},{9,13},{1... | collective-permute-start | bytes 589832 | tf_op jit(solution)/shard_map/ppermute | solution.py:428
  17.9 2.3 %collective-permute-start.5 = (bf16[4,64,384]{2,1,0:T(8,128)(2,1)S(1)}, bf16[4,64,384]{2,1,0:T(8,128)(2,1)S(1)}, u32[]{:S(2)}, u32[]{:S(2)}) collective-permute-start(bf16[4,64,384]{2,1,0:T(8,128)(2,1)S(1)} %get-tuple-element.39), channel_id=1, source_target_pairs={{4,0},{5,1},{6,2},{7,3},{8,4},{9,5},{10,6},{11,7},{12,8},{13,9},{1... | collective-permute-start | bytes 589832 | tf_op jit(solution)/shard_map/ppermute | solution.py:429
  20.2 0.1 all-to-all-done.stat_ref
  20.3 0.0 copy-done
  20.3 0.0 copy-done.1
  20.3 8.3 %frame0.1 = (bf16[360,384]{1,0:T(8,128)(2,1)S(1)}, bf16[60,8,384]{2,1,0:T(8,128)(2,1)S(1)}, bf16[3,1152,1152]{2,1,0:T(8,128)(2,1)S(1)}, f32[8,384]{1,0:T(8,128)S...) custom-call(f32[32,1,128]{2,1,0:T(1,128)S(1)} %all-to-all-done.stat_, ...), custom_call_target="tpu_custom_call" | custom-call | flops 10000000000 | bytes 30000000 | tf_op jit(solution)/shard_map/frame0/pallas_call | solution.py:431
  28.6 1.9 %collective-permute-start.2 = (bf16[360,384]{1,0:T(8,128)(2,1)S(1)}, bf16[360,384]{1,0:T(8,128)(2,1)S(1)}, u32[]{:S(2)}, u32[]{:S(2)}) collective-permute-start(bf16[360,384]{1,0:T(8,128)(2,1)S(1)} %get-tuple-element.27), channel_id=1, source_target_pairs={{0,32},{32,64},{64,96},{96,128},{128,160},{160,192},{192,224},{224... | collective-permute-start | bytes 829448 | tf_op jit(solution)/shard_map/ppermute | solution.py:438
  30.5 0.0 collective-permute-done.3.beyond_ref
  30.5 5.7 %frame1_first.1 = (bf16[360,384]{1,0:T(8,128)(2,1)S(1)}, bf16[60,8,384]{2,1,0:T(8,128)(2,1)S(1)}, bf16[10,64,1152]{2,1,0:T(8,128)(2,1)S(1)}) custom-call(bf16[2,60,8,384]{3,2,1,0:T(8,128)(2,1)S(1)} %get-tuple-element.28.x_ref, f32[4,8,384]{2,1,0:T(8,128)S(1)} %get-tuple-element.25.left_ref, f32[4,8,384]{2,1,0:T(8,128)S(1)} %get-tuple-element.26.right_ref, ...), custom_call_target="tpu_custom_call" | custom-call | flops 4000000000 | bytes 12000000 | tf_op jit(solution)/shard_map/frame1_first/pallas_call | solution.py:442
  36.3 1.7 %collective-permute-start.4 = (bf16[360,384]{1,0:T(8,128)(2,1)S(1)}, bf16[360,384]{1,0:T(8,128)(2,1)S(1)}, u32[]{:S(2)}, u32[]{:S(2)}) collective-permute-start(bf16[360,384]{1,0:T(8,128)(2,1)S(1)} %get-tuple-element.35), channel_id=1, source_target_pairs={{0,32},{32,64},{64,96},{96,128},{128,160},{160,192},{192,224},{224... | collective-permute-start | bytes 829448 | tf_op jit(solution)/shard_map/ppermute | solution.py:446
  38.0 0.0 collective-permute-done.5.beyond_ref
  38.0 3.9 %frame1_second.1 = bf16[240,384]{1,0:T(8,128)(2,1)S(1)} custom-call(bf16[2,60,8,384]{3,2,1,0:T(8,128)(2,1)S(1)} %get-tuple-element.28.x_ref, f32[4,8,384]{2,1,0:T(8,128)S(1)} %get-tuple-element.25.left_ref, f32[4,8,384]{2,1,0:T(8,128)S(1)} %get-tuple-element.26.right_ref, bf16[4,64,384]{2,1,0:T(8,128)(2,1)S(1)} %collective-permute-done.5.beyond_ref, ...), custom_call_target="tpu_custom_call" | custom-call | flops 4000000000 | bytes 12000000 | tf_op jit(solution)/shard_map/frame1_second/pallas_call | solution.py:447
  42.0 1.7 %collective-permute-start.6 = (bf16[240,384]{1,0:T(8,128)(2,1)S(1)}, bf16[240,384]{1,0:T(8,128)(2,1)S(1)}, u32[]{:S(2)}, u32[]{:S(2)}) collective-permute-start(bf16[240,384]{1,0:T(8,128)(2,1)S(1)} %frame1_second.1), channel_id=1, source_target_pairs={{0,32},{32,64},{64,96},{96,128},{128,160},{160,192},{192,224},{224... | collective-permute-start | bytes 552968 | tf_op jit(solution)/shard_map/ppermute | solution.py:451
  43.7 0.0 collective-permute-done.2.y0_ref
  43.7 3.2 %collective-permute-done.4.half_ref = bf16[360,384]{1,0:T(8,128)(2,1)S(1)} collective-permute-done((bf16[360,384]{1,0:T(8,128)(2,1)S(1)}, bf16[360,384]{1,0:T(8,128)(2,1)S(1)}, u32[]{:S(2)}, u32[]{:S(2)}) %collective-permute-start.4) | collective-permute-done | bytes 276512 | tf_op jit(solution)/shard_map/ppermute | solution.py:446
  46.9 1.0 %spread_rows.1 = (f32[2,3,480,128]{3,2,1,0:T(8,128)S(1)}, bf16[2,60,8,384]{3,2,1,0:T(8,128)(2,1)}) custom-call(bf16[360,384]{1,0:T(8,128)(2,1)S(1)} %collective-permute-done.2.y0_ref, bf16[360,384]{1,0:T(8,128)(2,1)S(1)} %collective-permute-done.4.half_ref, bf16[60,8,384]{2,1,0:T(8,128)(2,1)S(1)} %get-tuple-element.36.new0_ref, ...), custom_call_target="tpu_custom_call" | custom-call | flops 10000000000 | bytes 30000000 | tf_op jit(solution)/shard_map/spread_rows/pallas_call | solution.py:452
  47.9 2.9 %collective-permute-done.6.half_ref = bf16[240,384]{1,0:T(8,128)(2,1)S(1)} collective-permute-done((bf16[240,384]{1,0:T(8,128)(2,1)S(1)}, bf16[240,384]{1,0:T(8,128)(2,1)S(1)}, u32[]{:S(2)}, u32[]{:S(2)}) %collective-permute-start.6) | collective-permute-done | bytes 184352 | tf_op jit(solution)/shard_map/ppermute | solution.py:451
  50.8 1.1 %join_rows.1 = bf16[2,60,8,384]{3,2,1,0:T(8,128)(2,1)} custom-call(f32[2,3,480,128]{3,2,1,0:T(8,128)S(1)} %get-tuple-element.38.flat_ref, bf16[240,384]{1,0:T(8,128)(2,1)S(1)} %collective-permute-done.6.half_ref), custom_call_target="tpu_custom_call" | custom-call | flops 1000000000 | bytes 3000000 | tf_op jit(solution)/shard_map/join_rows/pallas_call | solution.py:456
Async XLA Ops:
  3.0 10.4 %collective-permute-start = (bf16[4,8,384]{2,1,0:T(8,128)(2,1)S(1)}, bf16[4,8,384]{2,1,0:T(8,128)(2,1)S(1)}, u32[]{:S(2)}, u32[]{:S(2)}) collective-permute-start(bf16[4,8,384]{2,1,0:T(8,128)(2,1)S(1)} %get-tuple-element.23), channel_id=1, source_target_pairs={{0,1},{1,2},{2,3},{3,0},{4,5},{5,6},{6,7},{7,4},{8,9},{9,10},{10,1... | collective-permute-start | bytes 73736 | tf_op jit(solution)/shard_map/ppermute | solution.py:422
  5.7 7.8 %collective-permute-start.1 = (bf16[4,8,384]{2,1,0:T(8,128)(2,1)S(1)}, bf16[4,8,384]{2,1,0:T(8,128)(2,1)S(1)}, u32[]{:S(2)}, u32[]{:S(2)}) collective-permute-start(bf16[4,8,384]{2,1,0:T(8,128)(2,1)S(1)} %get-tuple-element.24), channel_id=1, source_target_pairs={{1,0},{2,1},{3,2},{0,3},{5,4},{6,5},{7,6},{4,7},{9,8},{10,9},{11,1... | collective-permute-start | bytes 73736 | tf_op jit(solution)/shard_map/ppermute | solution.py:423
  6.4 13.9 %all-to-all-start = ((f32[32,1,128]{2,1,0:T(1,128)}), f32[32,1,128]{2,1,0:T(1,128)S(1)}, u32[]{:S(2)}, u32[]{:S(2)}) async-start(f32[32,1,128]{2,1,0:T(1,128)} %get-tuple-element.22), calls=%async_computation | async-start | bytes 32768 | tf_op jit(solution)/shard_map/all_to_all | solution.py:418
  13.4 6.9 %copy-start = (f32[1,384]{1,0:T(1,128)S(1)}, f32[1,384]{1,0:T(1,128)}, u32[]{:S(2)}) copy-start(f32[1,384]{1,0:T(1,128)} %bias_ref.5) | copy-start | bytes 4612
  13.4 6.9 %copy-start.1 = (f32[1,384]{1,0:T(1,128)S(1)}, f32[1,384]{1,0:T(1,128)}, u32[]{:S(2)}) copy-start(f32[1,384]{1,0:T(1,128)} %gain_ref.1) | copy-start | bytes 4612
  14.9 15.6 %collective-permute-start.3 = (bf16[4,64,384]{2,1,0:T(8,128)(2,1)S(1)}, bf16[4,64,384]{2,1,0:T(8,128)(2,1)S(1)}, u32[]{:S(2)}, u32[]{:S(2)}) collective-permute-start(bf16[4,64,384]{2,1,0:T(8,128)(2,1)S(1)} %get-tuple-element.29), channel_id=1, source_target_pairs={{0,4},{1,5},{2,6},{3,7},{4,8},{5,9},{6,10},{7,11},{8,12},{9,13},{1... | collective-permute-start | bytes 589832 | tf_op jit(solution)/shard_map/ppermute | solution.py:428
  17.9 20.1 %collective-permute-start.5 = (bf16[4,64,384]{2,1,0:T(8,128)(2,1)S(1)}, bf16[4,64,384]{2,1,0:T(8,128)(2,1)S(1)}, u32[]{:S(2)}, u32[]{:S(2)}) collective-permute-start(bf16[4,64,384]{2,1,0:T(8,128)(2,1)S(1)} %get-tuple-element.39), channel_id=1, source_target_pairs={{4,0},{5,1},{6,2},{7,3},{8,4},{9,5},{10,6},{11,7},{12,8},{13,9},{1... | collective-permute-start | bytes 589832 | tf_op jit(solution)/shard_map/ppermute | solution.py:429
  28.6 15.0 %collective-permute-start.2 = (bf16[360,384]{1,0:T(8,128)(2,1)S(1)}, bf16[360,384]{1,0:T(8,128)(2,1)S(1)}, u32[]{:S(2)}, u32[]{:S(2)}) collective-permute-start(bf16[360,384]{1,0:T(8,128)(2,1)S(1)} %get-tuple-element.27), channel_id=1, source_target_pairs={{0,32},{32,64},{64,96},{96,128},{128,160},{160,192},{192,224},{224... | collective-permute-start | bytes 829448 | tf_op jit(solution)/shard_map/ppermute | solution.py:438
  36.3 10.6 %collective-permute-start.4 = (bf16[360,384]{1,0:T(8,128)(2,1)S(1)}, bf16[360,384]{1,0:T(8,128)(2,1)S(1)}, u32[]{:S(2)}, u32[]{:S(2)}) collective-permute-start(bf16[360,384]{1,0:T(8,128)(2,1)S(1)} %get-tuple-element.35), channel_id=1, source_target_pairs={{0,32},{32,64},{64,96},{96,128},{128,160},{160,192},{192,224},{224... | collective-permute-start | bytes 829448 | tf_op jit(solution)/shard_map/ppermute | solution.py:446
  42.0 8.9 %collective-permute-start.6 = (bf16[240,384]{1,0:T(8,128)(2,1)S(1)}, bf16[240,384]{1,0:T(8,128)(2,1)S(1)}, u32[]{:S(2)}, u32[]{:S(2)}) collective-permute-start(bf16[240,384]{1,0:T(8,128)(2,1)S(1)} %frame1_second.1), channel_id=1, source_target_pairs={{0,32},{32,64},{64,96},{96,128},{128,160},{160,192},{192,224},{224... | collective-permute-start | bytes 552968 | tf_op jit(solution)/shard_map/ppermute | solution.py:451
